TPU v7x, 32 devices: a whole 2x2x4 slice. The times are simulated.
32 devices in a mesh: row: 4 (over y, core), col: 4 (over z), dp: 2 (over x).
Axes of the slice: x: 2, y: 2, z: 4, core: 2. Of those that a mesh axis runs over, the one named last changes fastest.
Arguments:
- pair: bfloat16 [2, 64, 512, 512], P('dp', None, 'row', 'col'), may hold values from -120 to 120
- cotangent: bfloat16 [2, 64, 512, 512], P('dp', None, 'row', 'col'), may hold values from -6 to 6
- chain: int32 [2, 512], P('dp'), may hold values from 0 to 3, never falling along the last dimension, each value on 1 to 256 neighbouring positions
- dilation: int32 [2], replicated, may hold values from 1 to 8, as said below
- w_one: bfloat16 [9, 64, 64], replicated, may hold values from -0.25 to 0.25
- w_two: bfloat16 [9, 64, 64], replicated, may hold values from -0.25 to 0.25
- gain_one: float32 [64], replicated, may hold values from 0.25 to 1.75
- gain_two: float32 [64], replicated, may hold values from 0.25 to 1.75
- inter_bias: float32 [64], replicated, may hold values from -4 to 4
Outputs:
- grad_w_one: float32 [9, 64, 64], replicated
- grad_w_two: float32 [9, 64, 64], replicated
- grad_gain_one: float32 [64], replicated
- grad_gain_two: float32 [64], replicated
- grad_inter: float32 [64], replicated
- loss: float32 [], replicated
Inputs may be any that keep to these rules, and one draw needn't show every extreme that they name: `dilation`: each entry is 1, 2, 4 or 8, and at least one entry is 8. chain numbers never fall along a complex's residues; each of the 4 chains has at most 256 residues.
All inputs are finite; a program needn't handle non-finite values.
Results may differ from a plain program's by a relative error of at most 0.0071.
Values may be sent and summed in bfloat16 or wider, within the bound.
A program may use at most 128 MiB of HBM per device.

v0:
```python
import jax
import jax.numpy as jnp
from jax import lax
from jax.sharding import PartitionSpec as P

kernel_reach = 8
eps = 1e-05


def padded(block, sides, width):
    for axis, dim in sides:
        count = lax.axis_size(axis)
        forward = [(i, i + 1) for i in range(count - 1)]
        backward = [(target, source) for source, target in forward]
        low = lax.ppermute(
            lax.slice_in_dim(block, block.shape[dim] - width, None, axis=dim), axis, forward
        )
        high = lax.ppermute(lax.slice_in_dim(block, 0, width, axis=dim), axis, backward)
        block = jnp.concatenate([low, block, high], axis=dim)
    return block


def elu(z):
    return jnp.where(z > 0, z, jnp.exp(jnp.minimum(z, 0.0)) - 1.0)


def elu_slope(z):
    return jnp.where(z > 0, 1.0, jnp.exp(jnp.minimum(z, 0.0)))


def kernel_tap_window(padded_input, first, second, input_shape):
    zero = jnp.int32(0)
    return lax.dynamic_slice(padded_input, (zero, first, second), input_shape)


def widen(values):
    return padded(values, (("row", 1), ("col", 2)), kernel_reach)


def dilated_convolve(padded_input, input_shape, kernel_weights, dilation_rate):
    chans = input_shape[0]
    total = jnp.zeros((chans, input_shape[1] * input_shape[2]), jnp.float32)
    for step in range(9):
        upper_triangle, left_padding = (step // 3 - 1, step % 3 - 1)
        window_slice = kernel_tap_window(
            padded_input,
            kernel_reach + dilation_rate * upper_triangle,
            kernel_reach + dilation_rate * left_padding,
            input_shape,
        )
        total = total + jnp.dot(
            kernel_weights[step],
            window_slice.reshape(chans, -1),
            preferred_element_type=jnp.float32,
        )
    return total.reshape(input_shape)


def convolve_backward(output_gradient, kernel_weights, dilation_rate):
    chans = output_gradient.shape[0]
    padded_input = widen(output_gradient)
    total = jnp.zeros((chans, output_gradient.shape[1] * output_gradient.shape[2]), jnp.float32)
    for step in range(9):
        upper_triangle, left_padding = (step // 3 - 1, step % 3 - 1)
        window_slice = kernel_tap_window(
            padded_input,
            kernel_reach - dilation_rate * upper_triangle,
            kernel_reach - dilation_rate * left_padding,
            output_gradient.shape,
        )
        total = total + jnp.dot(
            kernel_weights[step].T,
            window_slice.reshape(chans, -1),
            preferred_element_type=jnp.float32,
        )
    return total.reshape(output_gradient.shape)


def kernel_weight_gradient(output_gradient, padded_input, dilation_rate):
    chans = output_gradient.shape[0]
    flat = output_gradient.reshape(chans, -1)
    result = []
    for step in range(9):
        upper_triangle, left_padding = (step // 3 - 1, step % 3 - 1)
        window_slice = kernel_tap_window(
            padded_input,
            kernel_reach + dilation_rate * upper_triangle,
            kernel_reach + dilation_rate * left_padding,
            output_gradient.shape,
        )
        result.append(
            lax.dot_general(
                flat,
                window_slice.reshape(chans, -1),
                (((1,), (1,)), ((), ())),
                preferred_element_type=jnp.float32,
            )
        )
    return jnp.stack(result)


def paired_total(first, second):
    return lax.psum((first, second), ("row", "col"))


def normalize(values, count):
    totals = paired_total(jnp.sum(values, axis=(1, 2)), jnp.sum(values * values, axis=(1, 2)))
    mean = totals[0] / count
    var = totals[1] / count - mean * mean
    centred = values - mean[:, None, None]
    return (centred * lax.rsqrt(var + eps)[:, None, None], var)


def local(pair, cotangent, chain, dilation, w_one, w_two, gain_one, gain_two, inter_bias):
    chans, side = (pair.shape[1], pair.shape[2])
    groups = lax.axis_size("row")
    length = side * groups
    count = float(length * length)
    stacked = pair.reshape(1, 1, chans, side, side)
    sectioned = lax.all_to_all(
        lax.all_to_all(stacked, "row", split_axis=3, concat_axis=0, tiled=True),
        "col",
        split_axis=0,
        concat_axis=1,
        tiled=True,
    )
    landed = lax.all_to_all(sectioned, "row", split_axis=1, concat_axis=0, tiled=True)
    pieces = landed.reshape(groups, chans, side // groups, side)
    mirrored = jnp.swapaxes(jnp.transpose(pieces, (1, 0, 2, 3)).reshape(chans, side, side), 1, 2)
    tile = pair[0]
    sym = ((tile.astype(jnp.float32) + mirrored.astype(jnp.float32)) * 0.5).astype(jnp.bfloat16)
    wide = sym.astype(jnp.float32)
    norm_one, var_one = normalize(wide, count)
    z_one = gain_one[:, None, None] * norm_one
    act_one = elu(z_one).astype(jnp.bfloat16)
    row_ids = lax.dynamic_slice_in_dim(chain[0], lax.axis_index("row") * side, side)
    col_ids = lax.dynamic_slice_in_dim(chain[0], lax.axis_index("col") * side, side)
    cross = (row_ids[:, None] != col_ids[None, :]).astype(jnp.float32)
    padded_one = widen(act_one)
    hid = (
        dilated_convolve(padded_one, act_one.shape, w_one, dilation[0])
        + inter_bias[:, None, None] * cross[None]
    )
    norm_two, var_two = normalize(hid, count)
    z_two = gain_two[:, None, None] * norm_two
    act_two = elu(z_two).astype(jnp.bfloat16)
    padded_two = widen(act_two)
    upd = dilated_convolve(padded_two, act_two.shape, w_two, dilation[1])
    cot_wide = cotangent[0].astype(jnp.float32)
    loss = jnp.sum((wide + upd) * cot_wide) / length
    g_upd = (cot_wide / length).astype(jnp.bfloat16)
    grad_two = kernel_weight_gradient(g_upd, padded_two, dilation[1])
    d_act_two = convolve_backward(g_upd, w_two, dilation[1])
    d_z_two = d_act_two * elu_slope(z_two)
    grad_g_two = jnp.sum(d_z_two * norm_two, axis=(1, 2))
    d_norm_two = d_z_two * gain_two[:, None, None]
    sums = paired_total(
        jnp.sum(d_norm_two, axis=(1, 2)), jnp.sum(d_norm_two * norm_two, axis=(1, 2))
    )
    mean_a = sums[0] / count
    mean_b = sums[1] / count
    d_hid = (d_norm_two - mean_a[:, None, None] - norm_two * mean_b[:, None, None]) * lax.rsqrt(
        var_two + eps
    )[:, None, None]
    grad_int = jnp.sum(d_hid * cross[None], axis=(1, 2))
    d_hid_low = d_hid.astype(jnp.bfloat16)
    grad_one = kernel_weight_gradient(d_hid_low, padded_one, dilation[0])
    d_act_one = convolve_backward(d_hid_low, w_one, dilation[0])
    grad_g_one = jnp.sum(d_act_one * elu_slope(z_one) * norm_one, axis=(1, 2))
    totals = lax.psum(
        (grad_one, grad_two, grad_g_one, grad_g_two, grad_int, loss), ("row", "col", "dp")
    )
    return (totals[0], totals[1], totals[2], totals[3], totals[4], totals[5])


def solution(mesh):
    in_specs = (
        P("dp", None, "row", "col"),
        P("dp", None, "row", "col"),
        P("dp", None),
        P(),
        P(),
        P(),
        P(),
        P(),
        P(),
    )
    out_specs = (P(), P(), P(), P(), P(), P())
    return jax.shard_map(local, mesh=mesh, in_specs=in_specs, out_specs=out_specs, check_vma=False)
```

profile of v0, /device:TPU:0, one launch (start us, length us, event | category | flops | bytes accessed | tf_op | source)
XLA Modules:
  0.0 701.5 jit_solution(5183082801833041562)
XLA Ops:
  7.2 4.3 copy.340
  11.5 4.6 all-to-all-start
  20.3 3.0 collective-permute-start
  23.6 18.8 %all-to-all-done = bf16[1,1,64,128,128]{4,2,1,0,3:T(8,128)(2,1)} async-done(((bf16[1,1,64,128,128]{4,2,1,0,3:T(8,128)(2,1)}), bf16[1,1,64,128,128]{4,2,1,0,3:T(8,128)(2,1)}, u32[]{:S(2)}, u32[]{:S(2)}) %all-to-all-start) | async-done | bytes 2097184 | tf_op jit(solution)/shard_map/all_to_all | solution.py:121
  42.4 4.3 copy.339
  46.7 5.8 all-to-all-start.1
  52.6 4.3 fusion.4
  63.9 4.3 copy.72
  68.6 3.4 fusion.361
  72.0 3.9 copy.65
  77.3 3.9 copy.64
  81.2 5.3 collective-permute-start.2
  86.6 4.2 copy.67
  91.9 5.0 copy.66
  96.9 8.6 %pad_maximum_fusion = bf16[64,144,144]{2,0,1:T(8,128)(2,1)} fusion(bf16[64,144,8]{2,0,1:T(8,128)(2,1)} %copy.67, bf16[64,8,128]{2,0,1:T(8,128)(2,1)S(1)} %collective-permute-done.1, bf16[64,128,128]{2,0,1:T(8,128)(2,1)S(1)} %fusion.2, bf16[64,8,128]{2,0,1:T(8,128)(2,1)S(1)} %collective-permute-done, bf16[64,144,8]{2,0,1:T(8,128)(2,1)} %copy.66), kind=kLoop, calls=%fused_computation.46 | loop fusion | flops 13271040 | bytes 5308416 | tf_op jit(solution)/shard_map/concatenate | solution.py:19
  105.5 21.0 %dynamic-slice_bitcast_fusion.8 = (bf16[128,8,8,128]{3,2,1,0:T(8,128)(2,1)}, bf16[128,8,8,128]{3,2,1,0:T(8,128)(2,1)}, bf16[128,8,8,128]{3,2,1,0:T(8,128)(2,1)},...) fusion(bf16[64,144,144]{2,0,1:T(8,128)(2,1)} %pad_maximum_fusio, ...), kind=kLoop, calls=%fused_computation.182 | loop fusion | bytes 33554440
  130.9 4.6 all-to-all-start.2
  135.7 3.1 convolution_add_fusion.30
  145.0 16.2 %all-to-all-done.2 = bf16[1,4,64,32,128]{4,3,2,0,1:T(8,128)(2,1)} async-done(((bf16[1,4,64,32,128]{4,3,2,0,1:T(8,128)(2,1)}), bf16[1,4,64,32,128]{4,3,2,0,1:T(8,128)(2,1)}, u32[]{:S(2)}, u32[]{:S(2)}) %all-to-all-start.2) | async-done | bytes 2097184 | tf_op jit(solution)/shard_map/all_to_all | solution.py:127
  161.2 4.1 bitcast_convert_fusion
  165.4 5.5 copy.82
  170.9 5.2 convert_reduce_fusion
  176.1 48.7 %all-reduce.4 = (f32[64]{0:T(128)S(1)}, f32[64]{0:T(128)S(1)}) all-reduce(f32[64]{0:T(128)S(1)} %get-tuple-element.14, f32[64]{0:T(128)S(1)} %get-tuple-element.13), channel_id=1, replica_groups=mesh['row'=4,'col'=4,'dp'=2] {'row','col'}, use_global_device_ids=true, to_apply=%region_3.0 | all-reduce | flops 128 | bytes 1024 | tf_op jit(solution)/shard_map/psum | solution.py:103
  224.8 3.3 fusion.5
  229.4 3.0 collective-permute-start.4
  232.5 4.3 convolution_add_fusion.26
  237.1 3.3 fusion.360
  240.4 3.9 copy.84
  245.9 3.9 copy.83
  249.8 5.3 collective-permute-start.6
  255.1 5.5 convolution_add_fusion.25
  260.6 4.1 copy.86
  264.8 5.0 copy.85
  269.8 8.6 %pad_maximum_fusion.1 = bf16[64,144,144]{2,0,1:T(8,128)(2,1)} fusion(bf16[64,144,8]{2,0,1:T(8,128)(2,1)} %copy.86, bf16[64,8,128]{2,0,1:T(8,128)(2,1)S(1)} %collective-permute-done.5, bf16[64,128,128]{2,0,1:T(8,128)(2,1)S(1)} %fusion.5, bf16[64,8,128]{2,0,1:T(8,128)(2,1)S(1)} %collective-permute-done.4, bf16[64,144,8]{2,0,1:T(8,128)(2,1)} %copy.85), kind=kLoop, calls=%fused_computation.47 | loop fusion | flops 13271040 | bytes 5308416 | tf_op jit(solution)/shard_map/concatenate | solution.py:19
  278.4 20.6 %dynamic-slice_bitcast_fusion.22 = (bf16[128,8,8,128]{3,2,1,0:T(8,128)(2,1)}, bf16[128,8,8,128]{3,2,1,0:T(8,128)(2,1)S(1)}, bf16[128,8,8,128]{3,2,1,0:T(8,128)(2...) fusion(bf16[64,144,144]{2,0,1:T(8,128)(2,1)} %pad_maximum_fusio, ...), kind=kLoop, calls=%fused_computation.211 | loop fusion | bytes 33554440
  312.4 3.4 fusion.28
  315.8 29.7 %all-reduce.3 = (f32[64]{0:T(128)S(1)}, f32[64]{0:T(128)S(1)}) all-reduce(f32[64]{0:T(128)S(1)} %get-tuple-element.10, f32[64]{0:T(128)S(1)} %get-tuple-element.9), channel_id=1, replica_groups=mesh['row'=4,'col'=4,'dp'=2] {'row','col'}, use_global_device_ids=true, to_apply=%region_7.8 | all-reduce | flops 128 | bytes 1024 | tf_op jit(solution)/shard_map/psum | solution.py:103
  345.5 7.1 %multiply_reduce_fusion.1 = (f32[64]{0:T(128)}, f32[64]{0:T(128)S(1)}, f32[64]{0:T(128)S(1)}, f32[16384,64]{0,1:T(8,128)}) fusion(f32[64]{0:T(128)S(1)} %copy-done.51, f32[64]{0:T(128)S(1)} %get-tuple-element.84, f32[64]{0:T(128)S(1)} %get-tuple-element.83, f32[16384]{0:T(1024)S(1)} %fusion.247, f32[64]{0:T(128)S(1)} %copy-done.48, ...), kind=kOutput, calls=%fused_computation.80 | convolution fusion | flops 150994752 | bytes 14764800 | tf_op jit(solution)/shard_map/dot_general | solution.py:71
  352.5 32.1 %all-reduce.2 = (f32[64]{0:T(128)S(1)}, f32[64]{0:T(128)S(1)}) all-reduce(f32[64]{0:T(128)S(1)} %get-tuple-element.8, f32[64]{0:T(128)S(1)} %get-tuple-element.7), channel_id=1, replica_groups=mesh['row'=4,'col'=4,'dp'=2] {'row','col'}, use_global_device_ids=true, to_apply=%region_11.12 | all-reduce | flops 128 | bytes 1024 | tf_op jit(solution)/shard_map/psum | solution.py:103
  384.6 7.4 %multiply_reduce_fusion = (f32[64]{0:T(128)}, bf16[64,16384]{1,0:T(8,128)(2,1)}, bf16[8,128,8,128]{3,2,1,0:T(8,128)(2,1)}) fusion(f32[16384]{0:T(1024)S(1)} %fusion.247, f32[64]{0:T(128)S(1)} %get-tuple-element.91, f32[64]{0:T(128)S(1)} %get-tuple-element.92, f32[64]{0:T(128)S(1)} %get-tuple-element.84, f32[64]{0:T(128)S(1)} %get-tuple-element.83, ...), kind=kLoop, calls=%fused_computation.79 | loop fusion | flops 20971456 | bytes 12650240 | tf_op jit(solution)/shard_map/reduce_sum | solution.py:165
  409.6 3.4 collective-permute-start.12
  413.3 3.3 fusion.359
  416.6 4.6 copy.99
  422.4 4.6 copy.98
  427.0 5.2 collective-permute-start.10
  432.6 3.3 fusion.358
  435.8 3.9 copy.104
  441.0 4.6 copy.103
  445.6 5.4 collective-permute-start.14
  451.0 5.0 copy.101
  456.0 5.0 copy.100
  461.1 7.7 %pad_maximum_fusion.2 = bf16[64,144,144]{2,0,1:T(8,128)(2,1)S(1)} fusion(bf16[64,144,8]{2,0,1:T(8,128)(2,1)} %copy.101, bf16[64,8,128]{2,0,1:T(8,128)(2,1)S(1)} %collective-permute-done.9, bf16[64,128,128]{2,0,1:T(8,128)(2,1)} %copy-done.7, bf16[64,8,128]{2,0,1:T(8,128)(2,1)S(1)} %collective-permute-done.8, bf16[64,144,8]{2,0,1:T(8,128)(2,1)} %copy.100), kind=kLoop, calls=%fused_computation.48 | loop fusion | flops 13271040 | bytes 5308416 | tf_op jit(solution)/shard_map/concatenate | solution.py:19
  472.7 21.5 %dynamic-slice_bitcast_fusion.16 = (bf16[128,8,8,128]{3,2,1,0:T(8,128)(2,1)}, bf16[128,8,8,128]{3,2,1,0:T(8,128)(2,1)}, bf16[128,8,8,128]{3,2,1,0:T(8,128)(2,1)}...) fusion(bf16[64,144,144]{2,0,1:T(8,128)(2,1)} %copy-done, ...), kind=kLoop, calls=%fused_computation.191 | loop fusion | bytes 33554440
  494.3 4.7 fusion.155
  499.0 3.5 fusion.215
  517.2 4.4 convolution_add_fusion.4
  523.6 4.2 copy.106
  527.7 5.0 copy.105
  532.7 8.6 %pad_maximum_fusion.3 = bf16[64,144,144]{2,0,1:T(8,128)(2,1)} fusion(bf16[64,144,8]{2,0,1:T(8,128)(2,1)} %copy.106, bf16[64,8,128]{2,0,1:T(8,128)(2,1)S(1)} %collective-permute-done.13, bf16[64,128,128]{2,0,1:T(8,128)(2,1)S(1)} %get-tuple-element.64, bf16[64,8,128]{2,0,1:T(8,128)(2,1)S(1)} %collective-permute-done.12, bf16[64,144,8]{2,0,1:T(8,128)(2,1)} %copy.105), kind=kLoop, calls=%fused_computation.49 | loop fusion | flops 13271040 | bytes 5308416 | tf_op jit(solution)/shard_map/concatenate | solution.py:19
  541.3 21.0 %dynamic-slice_bitcast_fusion = (bf16[128,8,8,128]{3,2,1,0:T(8,128)(2,1)}, bf16[128,8,8,128]{3,2,1,0:T(8,128)(2,1)}, bf16[128,8,8,128]{3,2,1,0:T(8,128)(2,1)}, b...) fusion(bf16[64,144,144]{2,0,1:T(8,128)(2,1)} %pad_maximum_fusio, ...), kind=kLoop, calls=%fused_computation.173 | loop fusion | bytes 33554440
  565.2 3.6 convolution_add_fusion.3
  588.4 3.4 fusion.3
  592.4 37.8 %all-reduce = (f32[64]{0:T(128)}, f32[64]{0:T(128)}, f32[64]{0:T(128)}, f32[]{:T(128)}) all-reduce(f32[64]{0:T(128)S(1)} %get-tuple-element.12, f32[64]{0:T(128)S(1)} %copy-done.58, f32[64]{0:T(128)S(1)} %copy-done.55, f32[]{:T(128)S(6)} %div.41), channel_id=1, replica_groups=mesh['row'=4,'col'=4,'dp'=2] {'row','col','dp'}, use_global_device_ids=true, to_apply=%region_15.16 | all-reduce | flops 193 | bytes 1544 | tf_op jit(solution)/shard_map/psum | solution.py:170
  630.3 60.9 %all-reduce.7.cloned.1.call-done = (f32[9,64,64]{2,1,0:T(8,128)}, f32[9,64,64]{2,1,0:T(8,128)}) async-done(((f32[9,64,64]{2,1,0:T(8,128)}, f32[9,64,64]{2,1,0:T(8,128)}), (f32[9,64,64]{2,1,0:T(8,128)}, f32[9,64,64]{2,1,0:T(8,128)})) %all-reduce.7.cloned.1.call-update) | async-done | bytes 294928 | tf_op jit(solution)/shard_map/psum | solution.py:170
  (216 shorter events, 101.9 us)
Async XLA Ops:
  11.5 11.9 %copy-start.57 = (s32[1,512]{1,0:T(1,128)S(1)}, s32[1,512]{1,0:T(1,128)}, u32[]{:S(2)}) copy-start(s32[1,512]{1,0:T(1,128)} %param.11) | copy-start | bytes 6148
  11.5 31.0 %all-to-all-start = ((bf16[1,1,64,128,128]{4,2,1,0,3:T(8,128)(2,1)}), bf16[1,1,64,128,128]{4,2,1,0,3:T(8,128)(2,1)}, u32[]{:S(2)}, u32[]{:S(2)}) async-start(bf16[1,1,64,128,128]{4,2,1,0,3:T(8,128)(2,1)} %bitcast.515), calls=%async_computation | async-start | bytes 4194304 | tf_op jit(solution)/shard_map/all_to_all | solution.py:121
  19.0 49.2 %collective-permute-start.1 = (bf16[64,8,128]{2,0,1:T(8,128)(2,1)S(1)}, bf16[64,8,128]{2,0,1:T(8,128)(2,1)S(1)}, u32[]{:S(2)}, u32[]{:S(2)}) collective-permute-start(bf16[64,8,128]{2,0,1:T(8,128)(2,1)S(1)} %get-tuple-element.80), channel_id=1, source_target_pairs={{8,0},{16,8},{24,16},{9,1},{17,9},{25,17},{10,2},{18,10},{26,18},{... | collective-permute-start | bytes 393224 | tf_op jit(solution)/shard_map/ppermute | solution.py:18
  20.3 47.9 %collective-permute-start = (bf16[64,8,128]{2,0,1:T(8,128)(2,1)S(1)}, bf16[64,8,128]{2,0,1:T(8,128)(2,1)S(1)}, u32[]{:S(2)}, u32[]{:S(2)}) collective-permute-start(bf16[64,8,128]{2,0,1:T(8,128)(2,1)S(1)} %get-tuple-element.79), channel_id=1, source_target_pairs={{0,8},{8,16},{16,24},{1,9},{9,17},{17,25},{2,10},{10,18},{18,26},{... | collective-permute-start | bytes 393224 | tf_op jit(solution)/shard_map/ppermute | solution.py:15
  46.7 10.1 %copy-start.56 = (s32[2]{0:T(128)S(1)}, s32[2]{0:T(128)}, u32[]{:S(2)}) copy-start(s32[2]{0:T(128)} %param.12) | copy-start | bytes 28
  46.7 84.1 %all-to-all-start.1 = ((bf16[4,1,64,32,128]{4,3,2,1,0:T(8,128)(2,1)}), bf16[4,1,64,32,128]{4,3,2,1,0:T(8,128)(2,1)}, u32[]{:S(2)}, u32[]{:S(2)}) async-start(bf16[4,1,64,32,128]{4,3,2,1,0:T(8,128)(2,1)} %bitcast.520), calls=%async_computation.1 | async-start | bytes 4194304 | tf_op jit(solution)/shard_map/all_to_all | solution.py:120
  75.9 10.7 %collective-permute-start.3 = (bf16[64,144,8]{1,2,0:T(8,128)(2,1)S(1)}, bf16[64,144,8]{1,2,0:T(8,128)(2,1)S(1)}, u32[]{:S(2)}, u32[]{:S(2)}) collective-permute-start(bf16[64,144,8]{1,2,0:T(8,128)(2,1)S(1)} %copy.65), channel_id=1, source_target_pairs={{2,0},{4,2},{6,4},{3,1},{5,3},{7,5},{10,8},{12,10},{14,12},{11,9},... | collective-permute-start | bytes 442376 | tf_op jit(solution)/shard_map/ppermute | solution.py:18
  81.2 10.7 %collective-permute-start.2 = (bf16[64,144,8]{1,2,0:T(8,128)(2,1)S(1)}, bf16[64,144,8]{1,2,0:T(8,128)(2,1)}, u32[]{:S(2)}, u32[]{:S(2)}) collective-permute-start(bf16[64,144,8]{1,2,0:T(8,128)(2,1)S(1)} %copy.64), channel_id=1, source_target_pairs={{0,2},{2,4},{4,6},{1,3},{3,5},{5,7},{8,10},{10,12},{12,14},{9,11},... | collective-permute-start | bytes 442376 | tf_op jit(solution)/shard_map/ppermute | solution.py:15
  105.5 21.0 %copy-start.44 = (bf16[9,64,64]{2,1,0:T(8,128)(2,1)S(1)}, bf16[9,64,64]{2,1,0:T(8,128)(2,1)}, u32[]{:S(2)}) copy-start(bf16[9,64,64]{2,1,0:T(8,128)(2,1)} %param.14) | copy-start | bytes 221188
  130.9 4.9 copy-start.29
  130.9 30.3 %all-to-all-start.2 = ((bf16[1,4,64,32,128]{4,3,2,0,1:T(8,128)(2,1)}), bf16[1,4,64,32,128]{4,3,2,0,1:T(8,128)(2,1)}, u32[]{:S(2)}, u32[]{:S(2)}) async-start(bf16[1,4,64,32,128]{4,3,2,0,1:T(8,128)(2,1)} %bitcast.21), calls=%async_computation.2 | async-start | bytes 4194304 | tf_op jit(solution)/shard_map/all_to_all | solution.py:127
  135.5 555.6 %all-reduce.7.cloned.1.call-start = ((), (), s32[]{:S(2)}) async-start(), calls=%async_computation.3 | async-start | bytes 1179648 | tf_op jit(solution)/shard_map/psum | solution.py:170
  135.7 3.1 copy-start.27
  140.4 1.7 copy-start.26
  165.4 5.5 copy-start.39
  170.9 53.9 %copy-start.53 = (f32[64]{0:T(128)S(1)}, f32[64]{0:T(128)}, u32[]{:S(2)}) copy-start(f32[64]{0:T(128)} %param.15) | copy-start | bytes 772
  224.7 7.7 %copy-start.14 = (f32[16384,64]{0,1:T(8,128)S(1)}, f32[16384,64]{0,1:T(8,128)}, u32[]{:S(2)}) copy-start(f32[16384,64]{0,1:T(8,128)} %convolution_add_fusion.27) | copy-start | bytes 12582916
  224.8 80.6 %copy-start.49 = (f32[64]{0:T(128)}, f32[64]{0:T(128)S(1)}, u32[]{:S(2)}) copy-start(f32[64]{0:T(128)S(1)} %get-tuple-element.88) | copy-start | bytes 772
  228.1 41.7 %copy-start.4 = (bf16[64,128,128]{2,0,1:T(8,128)(2,1)}, bf16[64,128,128]{2,0,1:T(8,128)(2,1)S(1)}, u32[]{:S(2)}) copy-start(bf16[64,128,128]{2,0,1:T(8,128)(2,1)S(1)} %fusion.5) | copy-start | bytes 6291460
  228.1 8.7 %collective-permute-start.5 = (bf16[64,8,128]{2,0,1:T(8,128)(2,1)S(1)}, bf16[64,8,128]{2,0,1:T(8,128)(2,1)S(1)}, u32[]{:S(2)}, u32[]{:S(2)}) collective-permute-start(bf16[64,8,128]{2,0,1:T(8,128)(2,1)S(1)} %get-tuple-element.78), channel_id=1, source_target_pairs={{8,0},{16,8},{24,16},{9,1},{17,9},{25,17},{10,2},{18,10},{26,18},{... | collective-permute-start | bytes 393224 | tf_op jit(solution)/shard_map/ppermute | solution.py:18
  229.4 7.4 %collective-permute-start.4 = (bf16[64,8,128]{2,0,1:T(8,128)(2,1)S(1)}, bf16[64,8,128]{2,0,1:T(8,128)(2,1)S(1)}, u32[]{:S(2)}, u32[]{:S(2)}) collective-permute-start(bf16[64,8,128]{2,0,1:T(8,128)(2,1)S(1)} %get-tuple-element.77), channel_id=1, source_target_pairs={{0,8},{8,16},{16,24},{1,9},{9,17},{17,25},{2,10},{10,18},{18,26},{... | collective-permute-start | bytes 393224 | tf_op jit(solution)/shard_map/ppermute | solution.py:15
  244.2 16.4 %collective-permute-start.7 = (bf16[64,144,8]{1,2,0:T(8,128)(2,1)S(1)}, bf16[64,144,8]{1,2,0:T(8,128)(2,1)S(1)}, u32[]{:S(2)}, u32[]{:S(2)}) collective-permute-start(bf16[64,144,8]{1,2,0:T(8,128)(2,1)S(1)} %copy.84), channel_id=1, source_target_pairs={{2,0},{4,2},{6,4},{3,1},{5,3},{7,5},{10,8},{12,10},{14,12},{11,9},... | collective-permute-start | bytes 442376 | tf_op jit(solution)/shard_map/ppermute | solution.py:18
  249.8 14.9 %collective-permute-start.6 = (bf16[64,144,8]{1,2,0:T(8,128)(2,1)S(1)}, bf16[64,144,8]{1,2,0:T(8,128)(2,1)}, u32[]{:S(2)}, u32[]{:S(2)}) collective-permute-start(bf16[64,144,8]{1,2,0:T(8,128)(2,1)S(1)} %copy.83), channel_id=1, source_target_pairs={{0,2},{2,4},{4,6},{1,3},{3,5},{5,7},{8,10},{10,12},{12,14},{9,11},... | collective-permute-start | bytes 442376 | tf_op jit(solution)/shard_map/ppermute | solution.py:15
  278.4 20.6 %copy-start.45 = (bf16[9,64,64]{2,1,0:T(8,128)(2,1)S(1)}, bf16[9,64,64]{2,1,0:T(8,128)(2,1)}, u32[]{:S(2)}) copy-start(bf16[9,64,64]{2,1,0:T(8,128)(2,1)} %param.13) | copy-start | bytes 221188
  299.0 2.4 copy-start.38
  306.3 2.2 copy-start.34
  312.4 33.1 %copy-start.42 = (bf16[128,8,8,128]{3,2,1,0:T(8,128)(2,1)S(1)}, bf16[128,8,8,128]{3,2,1,0:T(8,128)(2,1)}, u32[]{:S(2)}) copy-start(bf16[128,8,8,128]{3,2,1,0:T(8,128)(2,1)} %get-tuple-element.54) | copy-start | bytes 6291460
  312.4 33.1 %copy-start.51 = (f32[64]{0:T(128)S(1)}, f32[64]{0:T(128)}, u32[]{:S(2)}) copy-start(f32[64]{0:T(128)} %param.16) | copy-start | bytes 772
  384.6 7.4 %copy-start.2 = (f32[16384,64]{0,1:T(8,128)S(1)}, f32[16384,64]{0,1:T(8,128)}, u32[]{:S(2)}) copy-start(f32[16384,64]{0,1:T(8,128)} %get-tuple-element.89) | copy-start | bytes 12582916
  384.6 7.4 %copy-start.15 = (f32[16384,64]{0,1:T(8,128)S(1)}, f32[16384,64]{0,1:T(8,128)}, u32[]{:S(2)}) copy-start(f32[16384,64]{0,1:T(8,128)} %get-tuple-element.90) | copy-start | bytes 12582916
  384.6 10.4 %slice-start = ((s8[4718592]{0:T(1024)(128)(4,1)}), s8[524288]{0:T(1024)(128)(4,1)S(1)}, s32[]{:S(2)}) async-start(s8[4718592]{0:T(1024)(128)(4,1)} %bitcast.516), calls=%async_computation.4 | async-start | bytes 1048576
  392.0 3.0 slice-start.1
  395.0 18.0 %copy-start.7 = (bf16[64,128,128]{2,0,1:T(8,128)(2,1)}, bf16[64,128,128]{2,0,1:T(8,128)(2,1)S(1)}, u32[]{:S(2)}) copy-start(bf16[64,128,128]{2,0,1:T(8,128)(2,1)S(1)} %get-tuple-element.63) | copy-start | bytes 6291460
  397.1 2.0 copy-start.5
  403.8 12.8 %copy-start.46 = (f32[9,64,64]{2,1,0:T(8,128)}, f32[9,64,64]{2,1,0:T(8,128)S(1)}, u32[]{:S(2)}) copy-start(f32[9,64,64]{2,1,0:T(8,128)S(1)} %fusion.197) | copy-start | bytes 442372
  403.9 9.1 %collective-permute-start.9 = (bf16[64,8,128]{2,0,1:T(8,128)(2,1)S(1)}, bf16[64,8,128]{2,0,1:T(8,128)(2,1)S(1)}, u32[]{:S(2)}, u32[]{:S(2)}) collective-permute-start(bf16[64,8,128]{2,0,1:T(8,128)(2,1)S(1)} %get-tuple-element.76), channel_id=1, source_target_pairs={{8,0},{16,8},{24,16},{9,1},{17,9},{25,17},{10,2},{18,10},{26,18},{... | collective-permute-start | bytes 393224 | tf_op jit(solution)/shard_map/ppermute | solution.py:18
  405.2 7.8 %collective-permute-start.8 = (bf16[64,8,128]{2,0,1:T(8,128)(2,1)S(1)}, bf16[64,8,128]{2,0,1:T(8,128)(2,1)S(1)}, u32[]{:S(2)}, u32[]{:S(2)}) collective-permute-start(bf16[64,8,128]{2,0,1:T(8,128)(2,1)S(1)} %get-tuple-element.75), channel_id=1, source_target_pairs={{0,8},{8,16},{16,24},{1,9},{9,17},{17,25},{2,10},{10,18},{18,26},{... | collective-permute-start | bytes 393224 | tf_op jit(solution)/shard_map/ppermute | solution.py:15
  408.3 24.0 %collective-permute-start.13 = (bf16[64,8,128]{2,0,1:T(8,128)(2,1)S(1)}, bf16[64,8,128]{2,0,1:T(8,128)(2,1)S(1)}, u32[]{:S(2)}, u32[]{:S(2)}) collective-permute-start(bf16[64,8,128]{2,0,1:T(8,128)(2,1)S(1)} %get-tuple-element.74), channel_id=1, source_target_pairs={{8,0},{16,8},{24,16},{9,1},{17,9},{25,17},{10,2},{18,10},{26,18},{... | collective-permute-start | bytes 393224 | tf_op jit(solution)/shard_map/ppermute | solution.py:18
  409.6 22.7 %collective-permute-start.12 = (bf16[64,8,128]{2,0,1:T(8,128)(2,1)S(1)}, bf16[64,8,128]{2,0,1:T(8,128)(2,1)S(1)}, u32[]{:S(2)}, u32[]{:S(2)}) collective-permute-start(bf16[64,8,128]{2,0,1:T(8,128)(2,1)S(1)} %get-tuple-element.73), channel_id=1, source_target_pairs={{0,8},{8,16},{16,24},{1,9},{9,17},{17,25},{2,10},{10,18},{18,26},{... | collective-permute-start | bytes 393224 | tf_op jit(solution)/shard_map/ppermute | solution.py:15
  421.2 29.8 %collective-permute-start.11 = (bf16[64,144,8]{1,2,0:T(8,128)(2,1)}, bf16[64,144,8]{1,2,0:T(8,128)(2,1)}, u32[]{:S(2)}, u32[]{:S(2)}) collective-permute-start(bf16[64,144,8]{1,2,0:T(8,128)(2,1)} %copy.99), channel_id=1, source_target_pairs={{2,0},{4,2},{6,4},{3,1},{5,3},{7,5},{10,8},{12,10},{14,12},{11,9},... | collective-permute-start | bytes 442376 | tf_op jit(solution)/shard_map/ppermute | solution.py:18
  427.0 29.0 %collective-permute-start.10 = (bf16[64,144,8]{1,2,0:T(8,128)(2,1)}, bf16[64,144,8]{1,2,0:T(8,128)(2,1)}, u32[]{:S(2)}, u32[]{:S(2)}) collective-permute-start(bf16[64,144,8]{1,2,0:T(8,128)(2,1)} %copy.98), channel_id=1, source_target_pairs={{0,2},{2,4},{4,6},{1,3},{3,5},{5,7},{8,10},{10,12},{12,14},{9,11},... | collective-permute-start | bytes 442376 | tf_op jit(solution)/shard_map/ppermute | solution.py:15
  439.7 83.8 %collective-permute-start.15 = (bf16[64,144,8]{1,2,0:T(8,128)(2,1)S(1)}, bf16[64,144,8]{1,2,0:T(8,128)(2,1)S(1)}, u32[]{:S(2)}, u32[]{:S(2)}) collective-permute-start(bf16[64,144,8]{1,2,0:T(8,128)(2,1)S(1)} %copy.104), channel_id=1, source_target_pairs={{2,0},{4,2},{6,4},{3,1},{5,3},{7,5},{10,8},{12,10},{14,12},{11,9},... | collective-permute-start | bytes 442376 | tf_op jit(solution)/shard_map/ppermute | solution.py:18
  445.6 82.1 %collective-permute-start.14 = (bf16[64,144,8]{1,2,0:T(8,128)(2,1)}, bf16[64,144,8]{1,2,0:T(8,128)(2,1)}, u32[]{:S(2)}, u32[]{:S(2)}) collective-permute-start(bf16[64,144,8]{1,2,0:T(8,128)(2,1)} %copy.103), channel_id=1, source_target_pairs={{0,2},{2,4},{4,6},{1,3},{3,5},{5,7},{8,10},{10,12},{12,14},{9,11},... | collective-permute-start | bytes 442376 | tf_op jit(solution)/shard_map/ppermute | solution.py:15
  461.1 7.8 %copy-start.10 = (bf16[1,64,128,128]{3,2,1,0:T(8,128)(2,1)S(1)}, bf16[1,64,128,128]{3,2,1,0:T(8,128)(2,1)}, u32[]{:S(2)}) copy-start(bf16[1,64,128,128]{3,2,1,0:T(8,128)(2,1)} %param.10) | copy-start | bytes 6291460
  468.8 2.1 copy-start
  494.2 4.8 copy-start.1
  494.2 8.3 %copy-start.11 = (bf16[1,64,128,128]{3,2,1,0:T(8,128)(2,1)S(1)}, bf16[1,64,128,128]{3,2,1,0:T(8,128)(2,1)}, u32[]{:S(2)}) copy-start(bf16[1,64,128,128]{3,2,1,0:T(8,128)(2,1)} %param.10) | copy-start | bytes 6291460
  494.3 8.3 %copy-start.43 = (bf16[8,128,8,128]{3,2,1,0:T(8,128)(2,1)S(1)}, bf16[8,128,8,128]{3,2,1,0:T(8,128)(2,1)}, u32[]{:S(2)}) copy-start(bf16[8,128,8,128]{3,2,1,0:T(8,128)(2,1)} %get-tuple-element.62) | copy-start | bytes 6291460
  506.5 3.7 copy-start.32
  515.0 2.2 copy-start.3
  515.0 2.2 copy-start.52
  523.5 17.8 %copy-start.47 = (f32[9,64,64]{2,1,0:T(8,128)}, f32[9,64,64]{2,1,0:T(8,128)S(1)}, u32[]{:S(2)}) copy-start(f32[9,64,64]{2,1,0:T(8,128)S(1)} %fusion.233) | copy-start | bytes 442372
  565.1 3.7 copy-start.18
  572.0 2.2 copy-start.6
  572.0 2.9 copy-start.25
  576.5 1.6 copy-start.23
  579.7 1.6 copy-start.22
  582.9 1.6 copy-start.20
  584.5 1.6 copy-start.19
  586.1 2.2 copy-start.12
  586.1 2.2 copy-start.50
  586.1 2.2 copy-start.54
  588.4 4.1 copy-start.55
  588.4 4.1 copy-start.58
  (17 other events, 27.1 us)
Sparse Core Ops, SparseCore 0:
  565.3 125.7 all-reduce.6
where the time goes:
time: 712 us; the launch traced here: 702 us
  local copies, waits for them, and re-layouts  212 us (30%)
  blocking collectives  148 us (21%)
  waiting for transfers between devices  97.1 us (14%)
  matrix products  93.5 us (13%)
  other arithmetic  68.4 us (10%)
  starting transfers between devices  59.9 us (8%)
  between operations  22.4 us (3%)
    unnamed x129, local copies, waits for them, and re-layouts  113 us
    psum x3, blocking collectives, paired_total(): return lax.psum((first, second), ('row', 'col'))  110 us
    psum x1, waiting for transfers between devices, local(): lax.psum((grad_one, grad_two, grad_g_one, grad_g_two, grad_int, loss), ('...  60.9 us
    psum x1, blocking collectives, local(): lax.psum((grad_one, grad_two, grad_g_one, grad_g_two, grad_int, loss), ('...  37.8 us
    dot_general x18, matrix products, convolve_backward(): jnp.dot(kernel_weights[step].T, window_slice.reshape(chans, -1), preferre...  37.6 us
    concatenate x8, other arithmetic, padded(): block = jnp.concatenate([low, block, high], axis=dim)  34.8 us
    ppermute x8, starting transfers between devices, padded(): lax.ppermute(lax.slice_in_dim(block, block.shape[dim] - width, None, axis...  33.8 us
    dot_general x18, matrix products, kernel_weight_gradient(): lax.dot_general(flat, window_slice.reshape(chans, -1), (((1,), (1,)), (()...  30.2 us
  transfers between devices with their start and end apart: 20, of which 4 were waited for; matrix products, arithmetic and copies ran while one was open for 30% of the time, Pallas kernels for 0%

commit v1 on v0

v1 whole, which is shorter than its diff:
```python
import functools

import jax
import jax.numpy as jnp
from jax import lax
from jax.experimental import pallas as pl
from jax.experimental.pallas import tpu as pltpu
from jax.sharding import PartitionSpec as P

reach = 8
eps = 1e-05
f32 = jnp.float32
bf16 = jnp.bfloat16
MESH = pl.DeviceIdType.MESH
vmem = pl.BlockSpec(memory_space=pltpu.VMEM)
smem = pl.BlockSpec(memory_space=pltpu.SMEM)
anyspace = pl.BlockSpec(memory_space=pl.ANY)
LIMIT = 56 * 1024 * 1024


def shape(dims, dtype):
    return jax.ShapeDtypeStruct(dims, dtype)


def lanes(chans=64, width=128):
    return lax.broadcasted_iota(jnp.int32, (chans, width), 1)


def pack_edges(rows, chans, side):
    group = lanes(chans, side) // reach
    low = jnp.zeros((chans, side), f32)
    high = jnp.zeros((chans, side), f32)
    for j, row in enumerate(rows):
        low = jnp.where(group == j, row if j == 0 else pltpu.roll(row, 8 * j, 1), low)
        shift = (8 * j + 8) % side
        high = jnp.where(group == j, row if shift == 0 else pltpu.roll(row, shift, 1), high)
    return low.astype(bf16), high.astype(bf16)


def as_columns(columns, chans, side):
    lane = lanes(chans, side)
    tile = jnp.zeros((chans, side), f32)
    for k, values in enumerate(columns):
        tile = jnp.where(lane == k, jnp.sum(values, axis=1, keepdims=True), tile)
    return tile


def edges_kernel(x_ref, low_ref, high_ref):
    side, chans = x_ref.shape[0], x_ref.shape[1]

    def body(k, carry):
        rows = [x_ref[16 * k + j].astype(f32) for j in range(16)]
        low_ref[k], high_ref[k] = pack_edges(rows, chans, side)
        return carry

    lax.fori_loop(0, side // 16, body, 0)


def sym_kernel(x_ref, m_ref, cot_ref, sym_ref, low_ref, high_ref, stat_ref):
    side, chans = x_ref.shape[0], x_ref.shape[1]

    def body(k, carry):
        one, two, three = carry
        rows = []
        for j in range(16):
            p = 16 * k + j
            sym = ((x_ref[p].astype(f32) + m_ref[p].astype(f32)) * 0.5).astype(bf16)
            sym_ref[p] = sym
            wide = sym.astype(f32)
            rows.append(wide)
            one = one + wide
            two = two + wide * wide
            three = three + wide * cot_ref[p].astype(f32)
        low_ref[k], high_ref[k] = pack_edges(rows, chans, side)
        return one, two, three

    zero = jnp.zeros((chans, side), f32)
    sums = lax.fori_loop(0, side // 16, body, (zero, zero, zero))
    stat_ref[...] = as_columns(sums, chans, side)


def halo_body(x_ref, low_ref, high_ref, top_ref, bot_ref, left_ref, right_ref, send, recv):
    rows, cols = lax.axis_size("row"), lax.axis_size("col")
    r, c = lax.axis_index("row"), lax.axis_index("col")
    up, down = lax.rem(r + rows - 1, rows), lax.rem(r + 1, rows)
    lef, rig = lax.rem(c + cols - 1, cols), lax.rem(c + 1, cols)
    side, blocks = x_ref.shape[0], low_ref.shape[0]
    moves = [
        (high_ref, left_ref.at[pl.ds(1, blocks)], r, rig),
        (low_ref, right_ref.at[pl.ds(1, blocks)], r, lef),
        (x_ref.at[pl.ds(side - reach, reach)], top_ref, down, c),
        (x_ref.at[pl.ds(0, reach)], bot_ref, up, c),
        (high_ref.at[pl.ds(blocks - 1, 1)], left_ref.at[pl.ds(0, 1)], down, rig),
        (high_ref.at[pl.ds(0, 1)], left_ref.at[pl.ds(blocks + 1, 1)], up, rig),
        (low_ref.at[pl.ds(blocks - 1, 1)], right_ref.at[pl.ds(0, 1)], down, lef),
        (low_ref.at[pl.ds(0, 1)], right_ref.at[pl.ds(blocks + 1, 1)], up, lef),
    ]
    return [
        pltpu.make_async_remote_copy(
            src_ref=src,
            dst_ref=dst,
            send_sem=send.at[n],
            recv_sem=recv.at[n],
            device_id={"row": to_row, "col": to_col},
            device_id_type=MESH,
        )
        for n, (src, dst, to_row, to_col) in enumerate(moves)
    ]


def halo_kernel(x_ref, low_ref, high_ref, top_ref, bot_ref, left_ref, right_ref, send, recv):
    rows, cols = lax.axis_size("row"), lax.axis_size("col")
    r, c = lax.axis_index("row"), lax.axis_index("col")
    barrier = pltpu.get_barrier_semaphore()
    for a in (-1, 0, 1):
        for b in (-1, 0, 1):
            if a or b:
                pl.semaphore_signal(
                    barrier,
                    inc=1,
                    device_id={
                        "row": lax.rem(r + rows + a, rows),
                        "col": lax.rem(c + cols + b, cols),
                    },
                    device_id_type=MESH,
                )
    pl.semaphore_wait(barrier, 8)
    copies = halo_body(x_ref, low_ref, high_ref, top_ref, bot_ref, left_ref, right_ref, send, recv)
    for copy in copies:
        copy.start()
    for copy in copies:
        copy.wait()


def halo(x, low, high, number):
    side, chans, width = x.shape
    blocks = low.shape[0]
    return pl.pallas_call(
        halo_kernel,
        name="halo",
        out_shape=[
            shape((reach, chans, width), bf16),
            shape((reach, chans, width), bf16),
            shape((blocks + 2, chans, width), bf16),
            shape((blocks + 2, chans, width), bf16),
        ],
        in_specs=[anyspace] * 3,
        out_specs=[anyspace] * 4,
        scratch_shapes=[pltpu.SemaphoreType.DMA((8,)), pltpu.SemaphoreType.DMA((8,))],
        compiler_params=pltpu.CompilerParams(collective_id=number, has_side_effects=True),
    )(x, low, high)


def peer_of(index, cols, depth):
    return {
        "row": index // (cols * depth),
        "col": lax.rem(index // depth, cols),
        "dp": lax.rem(index, depth),
    }


def greet(barrier, me, count, peer):
    def body(step, carry):
        to = lax.rem(me + step, count)
        pl.semaphore_signal(barrier, inc=1, device_id=peer(to), device_id_type=MESH)
        return carry

    lax.fori_loop(1, count, body, 0)
    pl.semaphore_wait(barrier, count - 1)


def stats_kernel(x_ref, out_ref, own, slots, send, recv):
    rows, cols = lax.axis_size("row"), lax.axis_size("col")
    count = rows * cols
    me = lax.axis_index("row") * cols + lax.axis_index("col")
    chans = x_ref.shape[0]

    def peer(index):
        return {"row": index // cols, "col": lax.rem(index, cols)}

    greet(pltpu.get_barrier_semaphore(), me, count, peer)
    own[...] = x_ref[...].T[0:8, :]

    def copy_to(step):
        return pltpu.make_async_remote_copy(
            src_ref=own,
            dst_ref=slots.at[me],
            send_sem=send.at[step],
            recv_sem=recv.at[me],
            device_id=peer(lax.rem(me + step, count)),
            device_id_type=MESH,
        )

    def copy_from(step):
        source = lax.rem(me + step, count)
        return pltpu.make_async_remote_copy(
            src_ref=own,
            dst_ref=slots.at[source],
            send_sem=send.at[step],
            recv_sem=recv.at[source],
            device_id=peer(source),
            device_id_type=MESH,
        )

    def start(step, carry):
        copy_to(step).start()
        return carry

    def land(step, carry):
        copy_to(step).wait_send()
        copy_from(step).wait_recv()
        return carry

    slots[me] = own[...]
    lax.fori_loop(1, count, start, 0)
    lax.fori_loop(1, count, land, 0)
    total = jnp.sum(slots[...], axis=0)
    filled = jnp.concatenate([total, jnp.zeros((x_ref.shape[1] - 8, chans), f32)], axis=0)
    out_ref[...] = filled.T


def all_stats(tile, number):
    count = lax.axis_size("row") * lax.axis_size("col")
    chans = tile.shape[0]
    return pl.pallas_call(
        stats_kernel,
        name="stats",
        out_shape=shape(tile.shape, f32),
        in_specs=[vmem],
        out_specs=vmem,
        scratch_shapes=[
            pltpu.VMEM((8, chans), f32),
            pltpu.VMEM((count, 8, chans), f32),
            pltpu.SemaphoreType.DMA((count,)),
            pltpu.SemaphoreType.DMA((count,)),
        ],
        compiler_params=pltpu.CompilerParams(collective_id=number, has_side_effects=True),
    )(tile)


def total_kernel(x_ref, out_ref, slots, send, recv, send_two, recv_two):
    rows, cols, depth = lax.axis_size("row"), lax.axis_size("col"), lax.axis_size("dp")
    count = rows * cols * depth
    me = (lax.axis_index("row") * cols + lax.axis_index("col")) * depth + lax.axis_index("dp")
    peer = functools.partial(peer_of, cols=cols, depth=depth)
    greet(pltpu.get_barrier_semaphore(), me, count, peer)

    def scatter(step, source):
        to = lax.rem(me + step, count)
        return pltpu.make_async_remote_copy(
            src_ref=x_ref.at[to],
            dst_ref=slots.at[source],
            send_sem=send.at[step],
            recv_sem=recv.at[source],
            device_id=peer(to),
            device_id_type=MESH,
        )

    def gather(step, source):
        to = lax.rem(me + step, count)
        return pltpu.make_async_remote_copy(
            src_ref=out_ref.at[source],
            dst_ref=out_ref.at[source],
            send_sem=send_two.at[step],
            recv_sem=recv_two.at[source],
            device_id=peer(to),
            device_id_type=MESH,
        )

    def run(make):
        def start(step, carry):
            make(step, me).start()
            return carry

        def land(step, carry):
            make(step, me).wait_send()
            make(step, lax.rem(me + step, count)).wait_recv()
            return carry

        lax.fori_loop(1, count, start, 0)
        lax.fori_loop(1, count, land, 0)

    slots[me] = x_ref[me]
    run(scatter)
    out_ref[me] = jnp.sum(slots[...], axis=0)
    run(gather)


def grand_total(flat, number):
    count = lax.axis_size("row") * lax.axis_size("col") * lax.axis_size("dp")
    rows = flat.shape[0]
    each = -(-rows // (8 * count)) * 8
    padded = jnp.pad(flat, ((0, each * count - rows), (0, 0))).reshape(count, each, 128)
    out = pl.pallas_call(
        total_kernel,
        name="total",
        out_shape=shape(padded.shape, f32),
        in_specs=[vmem],
        out_specs=vmem,
        scratch_shapes=[pltpu.VMEM(padded.shape, f32)] + [pltpu.SemaphoreType.DMA((count,))] * 4,
        compiler_params=pltpu.CompilerParams(
            collective_id=number, has_side_effects=True, vmem_limit_bytes=LIMIT
        ),
    )(padded)
    return out.reshape(each * count, 128)[:rows]


def stack_shifts(centre, left, right, out_ref, dil):
    height, chans, side = centre.shape
    lane = lanes(chans, side)

    def body(row, carry):
        block, j = (row + reach) // 16, lax.rem(row + reach, 16)
        x = centre[row].astype(f32)
        low = pltpu.roll(left[block], lax.rem(dil - 8 - 8 * j + 2 * side, side), 1)
        high = pltpu.roll(right[block], lax.rem(2 * side - dil - 8 * j, side), 1)
        before = jnp.where(lane < dil, low, pltpu.roll(x, dil, 1))
        after = jnp.where(lane >= side - dil, high, pltpu.roll(x, side - dil, 1))
        out_ref[row] = jnp.concatenate(
            [before.astype(bf16), centre[row], after.astype(bf16)], axis=0
        )
        return carry

    lax.fori_loop(0, height, body, 0, unroll=4)


def taps_of(stack_ref, p, dil, group):
    return jnp.concatenate(
        [
            jnp.concatenate(
                [stack_ref[p + k + reach + u * dil] for k in range(group)], axis=1
            )
            for u in (-1, 0, 1)
        ],
        axis=0,
    )


def backward_kernel(
    meta, x_ref, top, bot, left, right, w_ref, out_ref, stack_ref, centre, low, high, *, length
):
    side = x_ref.shape[0]
    dil = meta[0]
    keep = [meta[k].astype(f32) for k in range(1, 5)]
    centre[pl.ds(reach, side)] = x_ref[...]
    centre[pl.ds(0, reach)] = (top[...].astype(f32) * keep[0]).astype(bf16)
    centre[pl.ds(reach + side, reach)] = (bot[...].astype(f32) * keep[1]).astype(bf16)
    blocks = left.shape[0]
    for k in range(blocks):
        edge = keep[0] if k == 0 else keep[1] if k == blocks - 1 else 1.0
        low[k] = left[k].astype(f32) * (keep[2] * edge)
        high[k] = right[k].astype(f32) * (keep[3] * edge)
    stack_shifts(centre, low, high, stack_ref, dil)

    def body(step, carry):
        p = 4 * step
        got = jnp.dot(w_ref[...], taps_of(stack_ref, p, dil, 4), preferred_element_type=f32)
        for k in range(4):
            out_ref[p + k] = got[:, side * k : side * (k + 1)] * (1.0 / length)
        return carry

    lax.fori_loop(0, side // 4, body, 0)


def moments(stat, count):
    mean = stat[:, 0:1] / count
    var = stat[:, 1:2] / count - mean * mean
    return mean, lax.rsqrt(var + eps)


def forward_kernel(
    meta, ids, x_ref, top, bot, left, right, stat, gain, bias, col_ids, w_ref,
    hid_ref, act_ref, slope_ref, sums_ref,
    centre_a, centre_s, low_a, high_a, low_s, high_s, *, count,
):
    side, chans = x_ref.shape[0], x_ref.shape[1]
    dil = meta[0]
    keep = [meta[k].astype(f32) for k in range(1, 5)]
    mean, scale = moments(stat[...], count)
    mean = jnp.broadcast_to(mean, (chans, side))
    scale = jnp.broadcast_to(scale, (chans, side))
    gained = jnp.broadcast_to(gain[...], (chans, side))

    def activate(x):
        norm = (x.astype(f32) - mean) * scale
        z = gained * norm
        e = jnp.exp(jnp.minimum(z, 0.0))
        return jnp.where(z > 0, z, e - 1.0), jnp.where(z > 0, 1.0, e) * norm

    def inner(p, carry):
        a, s = activate(x_ref[p])
        centre_a[p + reach] = a.astype(bf16)
        centre_s[p + reach] = s.astype(bf16)
        return carry

    lax.fori_loop(0, side, inner, 0, unroll=4)
    for k in range(reach):
        a, s = activate(top[k])
        centre_a[k] = (a * keep[0]).astype(bf16)
        centre_s[k] = (s * keep[0]).astype(bf16)
        a, s = activate(bot[k])
        centre_a[reach + side + k] = (a * keep[1]).astype(bf16)
        centre_s[reach + side + k] = (s * keep[1]).astype(bf16)
    blocks = left.shape[0]
    for k in range(blocks):
        edge = keep[0] if k == 0 else keep[1] if k == blocks - 1 else 1.0
        a, s = activate(left[k])
        low_a[k] = a * (keep[2] * edge)
        low_s[k] = s * (keep[2] * edge)
        a, s = activate(right[k])
        high_a[k] = a * (keep[3] * edge)
        high_s[k] = s * (keep[3] * edge)
    stack_shifts(centre_a, low_a, high_a, act_ref, dil)
    stack_shifts(centre_s, low_s, high_s, slope_ref, dil)
    biased = jnp.broadcast_to(bias[...], (chans, side))
    cols = jnp.broadcast_to(col_ids[...], (chans, side))

    def body(step, carry):
        one, two = carry
        p = 4 * step
        got = jnp.dot(w_ref[...], taps_of(act_ref, p, dil, 4), preferred_element_type=f32)
        for k in range(4):
            hid = got[:, side * k : side * (k + 1)] + jnp.where(cols != ids[p + k], biased, 0.0)
            hid_ref[p + k] = hid
            one = one + hid
            two = two + hid * hid
        return one, two

    zero = jnp.zeros((chans, side), f32)
    sums_ref[...] = as_columns(lax.fori_loop(0, side // 4, body, (zero, zero)), chans, side)


def second_kernel(
    meta, hid_ref, dact_ref, stat, gain, stack_ref, sums_ref, grad_ref, act_ref, *, count
):
    side, chans = hid_ref.shape[0], hid_ref.shape[1]
    dil = meta[0]
    mean, scale = moments(stat[...], count)
    mean = jnp.broadcast_to(mean, (chans, side))
    scale = jnp.broadcast_to(scale, (chans, side))
    gained = jnp.broadcast_to(gain[...], (chans, side))
    grad_ref[...] = jnp.zeros_like(grad_ref)

    def body(step, carry):
        sums = list(carry)
        p = 4 * step
        acts = []
        for k in range(4):
            dact = dact_ref[p + k]
            norm = (hid_ref[p + k] - mean) * scale
            z = gained * norm
            e = jnp.exp(jnp.minimum(z, 0.0))
            act = jnp.where(z > 0, z, e - 1.0).astype(bf16)
            acts.append(act)
            dz = dact * jnp.where(z > 0, 1.0, e)
            dn = gained * dz
            sums[0] = sums[0] + dn
            sums[1] = sums[1] + dn * norm
            sums[2] = sums[2] + dz * norm
            sums[3] = sums[3] + act.astype(f32) * dact
        grad_ref[...] += lax.dot_general(
            taps_of(stack_ref, p, dil, 4),
            jnp.concatenate(acts, axis=1),
            (((1,), (1,)), ((), ())),
            preferred_element_type=f32,
        )
        return tuple(sums)

    zero = jnp.zeros((chans, side), f32)
    sums = lax.fori_loop(0, side // 4, body, (zero,) * 4)
    sums_ref[...] = as_columns(sums, chans, side)


def first_kernel(
    meta, ids, hid_ref, dact_ref, stat, stat_two, gain, col_ids, act_ref, slope_ref, w_ref,
    sums_ref, grad_ref, slope_grad, *, count,
):
    side, chans = hid_ref.shape[0], hid_ref.shape[1]
    dil = meta[0]
    mean, scale = moments(stat[...], count)
    mean = jnp.broadcast_to(mean, (chans, side))
    scale = jnp.broadcast_to(scale, (chans, side))
    gained = jnp.broadcast_to(gain[...], (chans, side))
    mean_a = jnp.broadcast_to(stat_two[:, 0:1] / count, (chans, side))
    mean_b = jnp.broadcast_to(stat_two[:, 1:2] / count, (chans, side))
    cols = jnp.broadcast_to(col_ids[...], (chans, side))
    grad_ref[...] = jnp.zeros_like(grad_ref)
    slope_grad[...] = jnp.zeros_like(slope_grad)

    def body(step, total):
        p = 4 * step
        lows = []
        for k in range(4):
            norm = (hid_ref[p + k] - mean) * scale
            z = gained * norm
            slope = jnp.where(z > 0, 1.0, jnp.exp(jnp.minimum(z, 0.0)))
            dn = gained * (dact_ref[p + k] * slope)
            dhid = (dn - mean_a - norm * mean_b) * scale
            total = total + jnp.where(cols != ids[p + k], dhid, 0.0)
            lows.append(dhid.astype(bf16))
        low = jnp.concatenate(lows, axis=1)
        dims = (((1,), (1,)), ((), ()))
        grad_ref[...] += lax.dot_general(
            taps_of(act_ref, p, dil, 4), low, dims, preferred_element_type=f32
        )
        slope_grad[...] += lax.dot_general(
            taps_of(slope_ref, p, dil, 4), low, dims, preferred_element_type=f32
        )
        return total

    total = lax.fori_loop(0, side // 4, body, jnp.zeros((chans, side), f32))
    gain_grad = jnp.zeros((chans, chans), f32)
    for t in range(9):
        part = pl.ds(t * chans, chans)
        gain_grad = gain_grad + slope_grad[part, :] * w_ref[part, :]
    lane = lanes(chans, side)
    sums_ref[...] = jnp.where(
        lane == 1, jnp.sum(gain_grad, axis=1, keepdims=True), as_columns([total], chans, side)
    )


def compute(kernel, name, outs, specs, scratch=()):
    return pl.pallas_call(
        kernel,
        name=name,
        out_shape=outs,
        in_specs=specs,
        out_specs=jax.tree.map(lambda _: vmem, outs),
        scratch_shapes=list(scratch),
        compiler_params=pltpu.CompilerParams(vmem_limit_bytes=LIMIT),
    )


def local(pair, cotangent, chain, dilation, w_one, w_two, gain_one, gain_two, inter_bias):
    chans, side = pair.shape[1], pair.shape[2]
    rows, cols = lax.axis_size("row"), lax.axis_size("col")
    length = side * rows
    count = float(length * length)
    blocks = side // 16
    height = side + 2 * reach
    r, c = lax.axis_index("row"), lax.axis_index("col")

    turned = jnp.transpose(pair[0], (2, 0, 1))
    mirrored = lax.ppermute(
        turned,
        ("row", "col"),
        [(i * cols + j, j * cols + i) for i in range(rows) for j in range(cols)],
    )
    cot = jnp.transpose(cotangent[0], (1, 0, 2))
    tile = jnp.transpose(pair[0], (1, 0, 2))

    keep = jnp.stack([r > 0, r < rows - 1, c > 0, c < cols - 1]).astype(jnp.int32)
    meta_one = jnp.concatenate([dilation[0:1], keep])
    meta_two = jnp.concatenate([dilation[1:2], keep])
    row_ids = lax.dynamic_slice_in_dim(chain[0], r * side, side)
    col_ids = lax.dynamic_slice_in_dim(chain[0], c * side, side)[None]
    gain_a, gain_b, bias = gain_one[:, None], gain_two[:, None], inter_bias[:, None]
    forward_w = jnp.transpose(w_one, (1, 0, 2)).reshape(chans, 9 * chans)
    backward_w = jnp.transpose(w_two[::-1], (2, 0, 1)).reshape(chans, 9 * chans)
    slope_w = jnp.transpose(w_one, (0, 2, 1)).reshape(9 * chans, chans).astype(f32)

    full = (side, chans, side)
    edge = shape((blocks, chans, side), bf16)
    stats = shape((chans, side), f32)
    stacked = shape((height, 3 * chans, side), bf16)
    centre = pltpu.VMEM((height, chans, side), bf16)
    border = pltpu.VMEM((blocks + 2, chans, side), f32)

    low, high = compute(edges_kernel, "edges", [edge, edge], [vmem])(cot)
    top, bot, left, right = halo(cot, low, high, 1)
    d_act, cot_stack = compute(
        functools.partial(backward_kernel, length=length),
        "backward",
        [shape(full, f32), stacked],
        [smem] + [vmem] * 6,
        [centre, border, border],
    )(meta_two, cot, top, bot, left, right, backward_w)

    sym, low, high, stat_one = compute(
        sym_kernel, "sym", [shape(full, bf16), edge, edge, stats], [vmem] * 3
    )(tile, mirrored, cot)
    top, bot, left, right = halo(sym, low, high, 2)
    all_one = all_stats(stat_one, 3)
    hid, act_stack, slope_stack, stat_two = compute(
        functools.partial(forward_kernel, count=count),
        "forward",
        [shape(full, f32), stacked, stacked, stats],
        [smem, smem] + [vmem] * 10,
        [centre, centre, border, border, border, border],
    )(meta_one, row_ids, sym, top, bot, left, right, all_one, gain_a, bias, col_ids, forward_w)
    all_two = all_stats(stat_two, 4)
    stat_three, grad_two = compute(
        functools.partial(second_kernel, count=count),
        "second",
        [stats, shape((9 * chans, chans), f32)],
        [smem] + [vmem] * 5,
        [pltpu.VMEM((8, 128), f32)],
    )(meta_two, hid, d_act, all_two, gain_b, cot_stack)
    all_three = all_stats(stat_three, 5)
    stat_four, grad_one = compute(
        functools.partial(first_kernel, count=count),
        "first",
        [stats, shape((9 * chans, chans), f32)],
        [smem, smem] + [vmem] * 9,
        [pltpu.VMEM((9 * chans, chans), f32)],
    )(
        meta_one, row_ids, hid, d_act, all_two, all_three, gain_b, col_ids, act_stack,
        slope_stack, slope_w,
    )

    loss = stat_one[:, 2] * (1.0 / length) + stat_three[:, 3]
    vectors = jnp.stack([stat_four[:, 1], stat_three[:, 2], stat_four[:, 0], loss])
    flat = jnp.concatenate(
        [grad_one.reshape(-1, 128), grad_two.reshape(-1, 128), vectors.reshape(-1, 128)]
    )
    total = grand_total(flat, 6)
    size = 9 * chans * chans // 128
    out_one = jnp.transpose(total[:size].reshape(9, chans, chans), (0, 2, 1))
    out_two = total[size : 2 * size].reshape(9, chans, chans)[::-1] * (1.0 / length)
    ends = total[2 * size :].reshape(4, chans)
    return out_one, out_two, ends[0], ends[1], ends[2], jnp.sum(ends[3])


def solution(mesh):
    in_specs = (
        P("dp", None, "row", "col"),
        P("dp", None, "row", "col"),
        P("dp", None),
        P(),
        P(),
        P(),
        P(),
        P(),
        P(),
    )
    out_specs = (P(), P(), P(), P(), P(), P())
    return jax.shard_map(local, mesh=mesh, in_specs=in_specs, out_specs=out_specs, check_vma=False)
```

time: 712 us -> 288 us (0.40); the launches traced: 702 us -> 288 us
  Pallas kernels: 0 us -> 255 us
  local copies, waits for them, and re-layouts: 212 us -> 23.6 us
  blocking collectives: 148 us -> 0 us
  waiting for transfers between devices: 97.1 us -> 0.01 us
  matrix products: 93.5 us -> 0 us
  other arithmetic: 68.4 us -> 5.65 us
  starting transfers between devices: 59.9 us -> 2.24 us
  between operations: 22.4 us -> 0.79 us
    pallas_call x0 -> x12, Pallas kernels: none -> 255 us  [the longest x3 70.3 us: all_stats(): pl.pallas_call(stats_kernel, name='stats', out_shape=shape(tile.shape, f3...]
    psum x4 -> x0, blocking collectives: 148 us -> none  [the longest x3 110 us: paired_total(): return lax.psum((first, second), ('row', 'col'))]
    unnamed x129 -> x24, local copies, waits for them, and re-layouts: 113 us -> 10 us
    dot_general x54 -> x0, matrix products: 93.5 us -> none  [the longest x18 37.6 us: convolve_backward(): jnp.dot(kernel_weights[step].T, window_slice.reshape(chans, -1), preferre...]
    psum x1 -> x0, waiting for transfers between devices: 60.9 us -> none  [local(): lax.psum((grad_one, grad_two, grad_g_one, grad_g_two, grad_int, loss), ('...]
    slice x17 -> x4, local copies, waits for them, and re-layouts: 47 us -> 3.27 us  [the longest x1 1.01 us: local(): stat_four[:, 1]]
    ppermute x16 -> x1, starting transfers between devices: 44.7 us -> 2.24 us  [local(): lax.ppermute(turned, ('row', 'col'), [(i * cols + j, j * cols + i) for i...]
    ppermute x8 -> x0, local copies, waits for them, and re-layouts: 37.4 us -> none  [the longest x4 20 us: padded(): lax.ppermute(lax.slice_in_dim(block, block.shape[dim] - width, None, axis...]
  transfers between devices with their start and end apart: 20 -> 1, of which waited for: 4 -> 0; matrix products, arithmetic and copies ran while one was open for 30% -> 5% of each run, Pallas kernels for 0% -> 23%
where the time goes in v1:
time: 288 us
  Pallas kernels  255 us (89%)
  local copies, waits for them, and re-layouts  23.6 us (8%)
  other arithmetic  5.65 us (2%)
    pallas_call x3, Pallas kernels, all_stats(): pl.pallas_call(stats_kernel, name='stats', out_shape=shape(tile.shape, f3...  70.3 us
    pallas_call x2, Pallas kernels, halo(): pl.pallas_call(halo_kernel, name='halo', out_shape=[shape((reach, chans,...  54 us
    pallas_call x1, Pallas kernels, local(): compute(functools.partial(forward_kernel, count=count), 'forward', [shape...  29.2 us
    pallas_call x1, Pallas kernels, grand_total(): pl.pallas_call(total_kernel, name='total', out_shape=shape(padded.shape,...  28.7 us
    pallas_call x1, Pallas kernels, local(): compute(functools.partial(first_kernel, count=count), 'first', [stats, sh...  25.2 us
    pallas_call x1, Pallas kernels, local(): compute(functools.partial(backward_kernel, length=length), 'backward', [s...  19 us
    pallas_call x1, Pallas kernels, local(): compute(functools.partial(second_kernel, count=count), 'second', [stats,...  18.7 us
    unnamed x24, local copies, waits for them, and re-layouts  10 us
  transfers between devices with their start and end apart: 1, of which 0 were waited for; matrix products, arithmetic and copies ran while one was open for 5% of the time, Pallas kernels for 23%

profile of v1, /device:TPU:0, one launch (start us, length us, event | category | flops | bytes accessed | tf_op | source)
XLA Modules:
  0.0 287.6 jit_solution(13572538855040089876)
XLA Ops:
  0.6 4.2 %copy.26 = bf16[1,64,128,128]{2,1,3,0:T(8,128)(2,1)} copy(bf16[1,64,128,128]{3,2,1,0:T(8,128)(2,1)} %param.9) | data formatting | bytes 4194304 | tf_op args[0]
  4.8 2.2 collective-permute-start
  7.0 0.0 copy-start
  7.0 4.4 %copy.40 = bf16[1,64,128,128]{3,1,2,0:T(8,128)(2,1)} copy(bf16[1,64,128,128]{3,2,1,0:T(8,128)(2,1)} %param.10) | data formatting | bytes 4194304 | tf_op args[1]
  11.4 0.0 copy-done
  11.4 0.0 copy-start.2
  11.4 0.0 copy-start.7
  11.4 0.0 copy-start.8
  11.5 2.7 copy.28.x_ref
  14.2 0.0 copy-start.4
  14.2 0.0 copy-start.9
  14.2 0.0 copy-done.2
  14.2 0.1 copy.29
  14.3 0.8 copy.32.w_ref
  15.1 0.0 copy-done.7
  15.1 0.7 copy.30.gain
  15.8 0.0 copy-done.8
  15.8 0.7 copy.31.bias
  16.5 3.9 %edges.1 = (bf16[8,64,128]{2,1,0:T(8,128)(2,1)}, bf16[8,64,128]{2,1,0:T(8,128)(2,1)}) custom-call(bf16[128,64,128]{2,1,0:T(8,128)(2,1)} %bitcast.40), custom_call_target="tpu_custom_call" | custom-call | tf_op jit(solution)/shard_map/edges/pallas_call | solution.py:569
  20.4 0.0 copy-done.4
  20.4 0.0 copy-start.6
  20.4 0.8 copy.33.w_ref
  21.2 0.0 copy-done.9
  21.2 0.7 copy.34.gain
  21.9 0.9 copy.35
  22.7 0.0 copy-start.10
  22.7 42.1 %halo.3 = (bf16[8,64,128]{2,1,0:T(8,128)(2,1)}, bf16[8,64,128]{2,1,0:T(8,128)(2,1)}, bf16[10,64,128]{2,1,0:T(8,128)(2,1)}, bf16[10,64,128]{2,1,0:T(8,128)(2,1)}) custom-call(bf16[128,64,128]{2,1,0:T(8,128)(2,1)} %bitcast.41, bf16[8,64,128]{2,1,0:T(8,128)(2,1)} %get-tuple-element.39.low_ref, bf16[8,64,128]{2,1,0:T(8,128)(2,1)} %get-tuple-element.40.high_ref), custom_call_target="tpu_custom_call" | custom-call | tf_op jit(solution)/shard_map/halo/pallas_call | solution.py:138
  64.8 0.1 add_convert_fusion
  64.9 0.0 copy-done.6
  64.9 0.6 fusion.1
  65.5 1.9 pad_add_fusion
  67.4 19.0 %backward.1 = (f32[128,64,128]{2,1,0:T(8,128)}, bf16[144,192,128]{2,1,0:T(8,128)(2,1)}) custom-call(s32[5]{0:T(128)} %get-tuple-element.67.meta, bf16[128,64,128]{2,1,0:T(8,128)(2,1)} %bitcast.42, bf16[8,64,128]{2,1,0:T(8,128)(2,1)} %get-tuple-element.41.top, bf16[8,64,128]{2,1,0:T(8,128)(2,1)} %get-tuple-element.42.bot, ...), custom_call_target="tpu_custom_call" | custom-call | tf_op jit(solution)/shard_map/backward/pallas_call | solution.py:571
  86.3 0.0 copy-done.10
  86.3 0.5 constant_dynamic-slice_fusion
  86.8 0.0 collective-permute-done.m_ref
  86.8 0.0 copy-start.1
  86.8 1.4 copy-done.1
  88.2 6.6 %sym.1 = (bf16[128,64,128]{2,1,0:T(8,128)(2,1)}, bf16[8,64,128]{2,1,0:T(8,128)(2,1)}, bf16[8,64,128]{2,1,0:T(8,128)(2,1)}, f32[64,128]{1,0:T(8,128)}) custom-call(bf16[128,64,128]{2,1,0:T(8,128)(2,1)} %copy.28.x_ref, bf16[128,64,128]{2,1,0:T(8,128)(2,1)} %copy-done.1, bf16[128,64,128]{2,1,0:T(8,128)(2,1)} %bitcast.43), custom_call_target="tpu_custom_call" | custom-call | tf_op jit(solution)/shard_map/sym/pallas_call | solution.py:579
  94.8 52.9 %stats.3.stat = f32[64,128]{1,0:T(8,128)} custom-call(f32[64,128]{1,0:T(8,128)} %get-tuple-element.37.x_ref), custom_call_target="tpu_custom_call" | custom-call | tf_op jit(solution)/shard_map/stats/pallas_call | solution.py:225
  147.8 11.9 %halo.2 = (bf16[8,64,128]{2,1,0:T(8,128)(2,1)}, bf16[8,64,128]{2,1,0:T(8,128)(2,1)}, bf16[10,64,128]{2,1,0:T(8,128)(2,1)}, bf16[10,64,128]{2,1,0:T(8,128)(2,1)}) custom-call(bf16[128,64,128]{2,1,0:T(8,128)(2,1)} %get-tuple-element.30.x_ref, bf16[8,64,128]{2,1,0:T(8,128)(2,1)} %get-tuple-element.31.low_ref, bf16[8,64,128]{2,1,0:T(8,128)(2,1)} %get-tuple-element.32.high_ref), custom_call_target="tpu_custom_call" | custom-call | tf_op jit(solution)/shard_map/halo/pallas_call | solution.py:138
  159.7 29.2 %forward.1 = (f32[128,64,128]{2,1,0:T(8,128)}, bf16[144,192,128]{2,1,0:T(8,128)(2,1)}, bf16[144,192,128]{2,1,0:T(8,128)(2,1)}, f32[64,128]{1,0:T(8,128)}) custom-call(s32[5]{0:T(128)} %get-tuple-element.66.meta, s32[128]{0:T(128)} %get-tuple-element.65.ids, bf16[128,64,128]{2,1,0:T(8,128)(2,1)} %get-tuple-element.30.x_ref, ...), custom_call_target="tpu_custom_call" | custom-call | tf_op jit(solution)/shard_map/forward/pallas_call | solution.py:584
  188.9 8.6 %stats.4.stat = f32[64,128]{1,0:T(8,128)} custom-call(f32[64,128]{1,0:T(8,128)} %get-tuple-element.46.x_ref), custom_call_target="tpu_custom_call" | custom-call | tf_op jit(solution)/shard_map/stats/pallas_call | solution.py:225
  197.5 0.0 copy-start.5
  197.5 18.7 %second.1 = (f32[64,128]{1,0:T(8,128)}, f32[576,64]{1,0:T(8,128)}) custom-call(s32[5]{0:T(128)} %get-tuple-element.67.meta, f32[128,64,128]{2,1,0:T(8,128)} %get-tuple-element.38.hid_ref, f32[128,64,128]{2,1,0:T(8,128)} %get-tuple-element.45.dact_ref, f32[64,128]{1,0:T(8,128)} %stats.4.stat, f32[64,1]{1,0:T(8,128)} %copy.34.gain, ...), custom_call_target="tpu_custom_call" | custom-call | tf_op jit(solution)/shard_map/second/pallas_call | solution.py:592
  216.2 8.7 %stats.5.stat_two = f32[64,128]{1,0:T(8,128)} custom-call(f32[64,128]{1,0:T(8,128)} %get-tuple-element.48.x_ref), custom_call_target="tpu_custom_call" | custom-call | tf_op jit(solution)/shard_map/stats/pallas_call | solution.py:225
  224.9 0.0 copy-done.5
  224.9 1.0 slice_reduce_fusion.1
  226.0 0.0 copy-start.3
  226.0 25.2 %first.1 = (f32[64,128]{1,0:T(8,128)}, f32[576,64]{1,0:T(8,128)}) custom-call(s32[5]{0:T(128)} %get-tuple-element.66.meta, s32[128]{0:T(128)} %get-tuple-element.65.ids, f32[128,64,128]{2,1,0:T(8,128)} %get-tuple-element.38.hid_ref, f32[128,64,128]{2,1,0:T(8,128)} %get-tuple-element.45.dact_ref, f32[64,128]{1,0:T(8,128)} %stats.4.stat, ...), custom_call_target="tpu_custom_call" | custom-call | tf_op jit(solution)/shard_map/first/pallas_call | solution.py:600
  251.2 1.1 reshape.77
  252.2 1.0 slice_reduce_fusion.2
  253.3 0.1 reshape.79
  253.4 0.0 copy-done.3
  253.4 0.1 reshape.78
  253.5 0.8 select_maximum_fusion
  254.2 28.7 %total.1 = f32[32,24,128]{2,1,0:T(8,128)} custom-call(f32[32,24,128]{2,1,0:T(8,128)} %bitcast.46), custom_call_target="tpu_custom_call" | custom-call | tf_op jit(solution)/shard_map/total/pallas_call | solution.py:294
  282.9 1.0 fusion
  283.9 0.1 reshape.81
  284.0 0.9 copy.37
  284.9 0.1 reshape.82
  285.0 0.7 reverse_multiply_fusion
  285.8 0.7 slice.62
  286.4 0.1 reshape.84
  286.5 1.1 slice_reduce_fusion.3
  (3 shorter events, 0.0 us)
Async XLA Ops:
  4.8 82.1 %collective-permute-start = (bf16[128,64,128]{2,1,0:T(8,128)(2,1)}, bf16[128,64,128]{2,1,0:T(8,128)(2,1)S(1)}, u32[]{:S(2)}, u32[]{:S(2)}) collective-permute-start(bf16[128,64,128]{2,1,0:T(8,128)(2,1)} %bitcast.45), channel_id=1, source_target_pairs={{0,0},{2,8},{4,16},{6,24},{8,2},{10,10},{12,18},{14,26},{16,4},{18... | collective-permute-start | bytes 6291464 | tf_op jit(solution)/shard_map/ppermute | solution.py:544
  7.0 4.4 %copy-start = (bf16[1,64,128,128]{3,2,1,0:T(8,128)(2,1)S(1)}, bf16[1,64,128,128]{3,2,1,0:T(8,128)(2,1)}, u32[]{:S(2)}) copy-start(bf16[1,64,128,128]{3,2,1,0:T(8,128)(2,1)} %param.9) | copy-start | bytes 6291460
  11.4 2.7 copy-start.2
  11.4 3.7 %copy-start.7 = (f32[64]{0:T(128)S(1)}, f32[64]{0:T(128)}, u32[]{:S(2)}) copy-start(f32[64]{0:T(128)} %param.15) | copy-start | bytes 772
  11.4 4.3 %copy-start.8 = (f32[64]{0:T(128)S(1)}, f32[64]{0:T(128)}, u32[]{:S(2)}) copy-start(f32[64]{0:T(128)} %param.17) | copy-start | bytes 772
  14.2 6.2 %copy-start.4 = (bf16[9,64,64]{2,1,0:T(8,128)(2,1)S(1)}, bf16[9,64,64]{2,1,0:T(8,128)(2,1)}, u32[]{:S(2)}) copy-start(bf16[9,64,64]{2,1,0:T(8,128)(2,1)} %param.14) | copy-start | bytes 221188
  14.2 7.0 %copy-start.9 = (f32[64]{0:T(128)S(1)}, f32[64]{0:T(128)}, u32[]{:S(2)}) copy-start(f32[64]{0:T(128)} %param.16) | copy-start | bytes 772
  20.4 44.5 %copy-start.6 = (s32[2]{0:T(128)S(1)}, s32[2]{0:T(128)}, u32[]{:S(2)}) copy-start(s32[2]{0:T(128)} %param.12) | copy-start | bytes 28
  22.7 63.6 %copy-start.10 = (s32[1,512]{1,0:T(1,128)S(1)}, s32[1,512]{1,0:T(1,128)}, u32[]{:S(2)}) copy-start(s32[1,512]{1,0:T(1,128)} %param.11) | copy-start | bytes 6148
  86.8 1.4 copy-start.1
  197.5 27.4 %copy-start.5 = (f32[64,128]{1,0:T(8,128)S(1)}, f32[64,128]{1,0:T(8,128)}, u32[]{:S(2)}) copy-start(f32[64,128]{1,0:T(8,128)} %get-tuple-element.37.x_ref) | copy-start | bytes 98308
  226.0 27.4 %copy-start.3 = (f32[576,64]{1,0:T(8,128)S(1)}, f32[576,64]{1,0:T(8,128)}, u32[]{:S(2)}) copy-start(f32[576,64]{1,0:T(8,128)} %get-tuple-element.52) | copy-start | bytes 442372

commit v2 on v1

--- a/solution.py
+++ b/solution.py
@@ -56,26 +56,30 @@
     lax.fori_loop(0, side // 16, body, 0)
 
 
-def sym_kernel(x_ref, m_ref, cot_ref, sym_ref, low_ref, high_ref, stat_ref):
+def sym_kernel(x_ref, first_ref, last_ref, cot_ref, sym_ref, low_ref, high_ref, stat_ref):
     side, chans = x_ref.shape[0], x_ref.shape[1]
-
-    def body(k, carry):
+    half = side // 2
+
+    def body(m_ref, base, k, carry):
         one, two, three = carry
         rows = []
         for j in range(16):
             p = 16 * k + j
-            sym = ((x_ref[p].astype(f32) + m_ref[p].astype(f32)) * 0.5).astype(bf16)
-            sym_ref[p] = sym
+            sym = ((x_ref[p + base].astype(f32) + m_ref[p].astype(f32)) * 0.5).astype(bf16)
+            sym_ref[p + base] = sym
             wide = sym.astype(f32)
             rows.append(wide)
             one = one + wide
             two = two + wide * wide
-            three = three + wide * cot_ref[p].astype(f32)
-        low_ref[k], high_ref[k] = pack_edges(rows, chans, side)
+            three = three + wide * cot_ref[p + base].astype(f32)
+        at = k + base // 16
+        low_ref[at], high_ref[at] = pack_edges(rows, chans, side)
         return one, two, three
 
     zero = jnp.zeros((chans, side), f32)
-    sums = lax.fori_loop(0, side // 16, body, (zero, zero, zero))
+    sums = (zero, zero, zero)
+    for m_ref, base in ((first_ref, 0), (last_ref, half)):
+        sums = lax.fori_loop(0, half // 16, functools.partial(body, m_ref, base), sums)
     stat_ref[...] = as_columns(sums, chans, side)
 
 
@@ -540,12 +544,6 @@
     height = side + 2 * reach
     r, c = lax.axis_index("row"), lax.axis_index("col")
 
-    turned = jnp.transpose(pair[0], (2, 0, 1))
-    mirrored = lax.ppermute(
-        turned,
-        ("row", "col"),
-        [(i * cols + j, j * cols + i) for i in range(rows) for j in range(cols)],
-    )
     cot = jnp.transpose(cotangent[0], (1, 0, 2))
     tile = jnp.transpose(pair[0], (1, 0, 2))
 
@@ -568,6 +566,21 @@
 
     low, high = compute(edges_kernel, "edges", [edge, edge], [vmem])(cot)
     top, bot, left, right = halo(cot, low, high, 1)
+    source, top = lax.optimization_barrier((pair[0], top))
+    turned = jnp.transpose(source, (2, 0, 1))
+    flip = 2 if rows % 4 == 0 else 1
+    pairs = [(i, j) for i in range(rows) for j in range(cols)]
+    aside = lax.ppermute(
+        turned[side // 2 :],
+        ("row", "col"),
+        [(i * cols + j, (i ^ flip) * cols + j) for i, j in pairs],
+    )
+    direct = lax.ppermute(
+        turned[: side // 2], ("row", "col"), [(i * cols + j, j * cols + i) for i, j in pairs]
+    )
+    onward = lax.ppermute(
+        aside, ("row", "col"), [((i ^ flip) * cols + j, j * cols + i) for i, j in pairs]
+    )
     d_act, cot_stack = compute(
         functools.partial(backward_kernel, length=length),
         "backward",
@@ -577,8 +590,8 @@
     )(meta_two, cot, top, bot, left, right, backward_w)
 
     sym, low, high, stat_one = compute(
-        sym_kernel, "sym", [shape(full, bf16), edge, edge, stats], [vmem] * 3
-    )(tile, mirrored, cot)
+        sym_kernel, "sym", [shape(full, bf16), edge, edge, stats], [vmem] * 4
+    )(tile, direct, onward, cot)
     top, bot, left, right = halo(sym, low, high, 2)
     all_one = all_stats(stat_one, 3)
     hid, act_stack, slope_stack, stat_two = compute(

time: 288 us -> 275 us (0.955)
  Pallas kernels: 255 us -> 198 us
  waiting for transfers between devices: 0.01 us -> 37.8 us
  starting transfers between devices: 2.24 us -> 7.45 us
    ppermute x1 -> x3, waiting for transfers between devices: 0.01 us -> 37.8 us  [the longest x1 37.8 us: local(): lax.ppermute(turned[side // 2:], ('row', 'col'), [(i * cols + j, (i ^ fli...]
    pallas_call x3, Pallas kernels: 70.3 us -> 41.2 us  [all_stats(): pl.pallas_call(stats_kernel, name='stats', out_shape=shape(tile.shape, f3...]
    pallas_call x2, Pallas kernels: 54 us -> 26.4 us  [halo(): pl.pallas_call(halo_kernel, name='halo', out_shape=[shape((reach, chans,...]
    ppermute x1 -> x3, starting transfers between devices: 2.24 us -> 7.45 us  [the longest x1 4.47 us: local(): lax.ppermute(aside, ('row', 'col'), [((i ^ flip) * cols + j, j * cols + i...]
  transfers between devices with their start and end apart: 1 -> 3, of which waited for: 0 -> 1; matrix products, arithmetic and copies ran while one was open for 5% -> 4% of each run, Pallas kernels for 23% -> 7%
where the time goes in v2:
time: 275 us; the launch traced here: 274 us
  Pallas kernels  198 us (72%)
  waiting for transfers between devices  37.8 us (14%)
  local copies, waits for them, and re-layouts  24.4 us (9%)
  starting transfers between devices  7.45 us (3%)
  other arithmetic  5.65 us (2%)
    pallas_call x3, Pallas kernels, all_stats(): pl.pallas_call(stats_kernel, name='stats', out_shape=shape(tile.shape, f3...  41.2 us
    ppermute x1, waiting for transfers between devices, local(): lax.ppermute(turned[side // 2:], ('row', 'col'), [(i * cols + j, (i ^ fli...  37.8 us
    pallas_call x1, Pallas kernels, local(): compute(functools.partial(forward_kernel, count=count), 'forward', [shape...  29.2 us
    pallas_call x1, Pallas kernels, grand_total(): pl.pallas_call(total_kernel, name='total', out_shape=shape(padded.shape,...  27.7 us
    pallas_call x2, Pallas kernels, halo(): pl.pallas_call(halo_kernel, name='halo', out_shape=[shape((reach, chans,...  26.4 us
    pallas_call x1, Pallas kernels, local(): compute(functools.partial(first_kernel, count=count), 'first', [stats, sh...  25.2 us
    pallas_call x1, Pallas kernels, local(): compute(functools.partial(backward_kernel, length=length), 'backward', [s...  18.9 us
    pallas_call x1, Pallas kernels, local(): compute(functools.partial(second_kernel, count=count), 'second', [stats,...  18.7 us
  transfers between devices with their start and end apart: 3, of which 1 were waited for; matrix products, arithmetic and copies ran while one was open for 4% of the time, Pallas kernels for 7%

profile of v2, /device:TPU:0, one launch (start us, length us, event | category | flops | bytes accessed | tf_op | source)
XLA Modules:
  0.0 274.1 jit_solution(1320175746322365696)
XLA Ops:
  0.6 4.3 %copy.40 = bf16[1,64,128,128]{3,1,2,0:T(8,128)(2,1)} copy(bf16[1,64,128,128]{3,2,1,0:T(8,128)(2,1)} %param.10) | data formatting | bytes 4194304 | tf_op args[1]
  5.0 0.0 copy-start
  5.0 4.0 %edges.1 = (bf16[8,64,128]{2,1,0:T(8,128)(2,1)}, bf16[8,64,128]{2,1,0:T(8,128)(2,1)}) custom-call(bf16[128,64,128]{2,1,0:T(8,128)(2,1)} %bitcast.39), custom_call_target="tpu_custom_call" | custom-call | tf_op jit(solution)/shard_map/edges/pallas_call | solution.py:567
  9.0 0.0 copy-done
  9.0 2.9 %copy.26 = bf16[1,64,128,128]{2,1,3,0:T(8,128)(2,1)} copy(bf16[1,64,128,128]{3,2,1,0:T(8,128)(2,1)S(1)} %copy-done) | data formatting | bytes 4194304 | tf_op args[0]
  11.9 14.4 %halo.2 = (bf16[8,64,128]{2,1,0:T(8,128)(2,1)}, bf16[8,64,128]{2,1,0:T(8,128)(2,1)}, bf16[10,64,128]{2,1,0:T(8,128)(2,1)}, bf16[10,64,128]{2,1,0:T(8,128)(2,1)}) custom-call(bf16[128,64,128]{2,1,0:T(8,128)(2,1)} %bitcast.40, bf16[8,64,128]{2,1,0:T(8,128)(2,1)} %get-tuple-element.32.low_ref, bf16[8,64,128]{2,1,0:T(8,128)(2,1)} %get-tuple-element.33.high_ref), custom_call_target="tpu_custom_call" | custom-call | tf_op jit(solution)/shard_map/halo/pallas_call | solution.py:142
  26.3 2.7 fusion
  29.0 1.1 collective-permute-start.1
  30.1 1.9 collective-permute-start
  32.0 37.8 %collective-permute-done.1 = bf16[64,64,128]{2,1,0:T(8,128)(2,1)} collective-permute-done((bf16[64,64,128]{2,1,0:T(8,128)(2,1)S(1)}, bf16[64,64,128]{2,1,0:T(8,128)(2,1)}, u32[]{:S(2)}, u32[]{:S(2)}) %collective-permute-start.1) | collective-permute-done | bytes 1048608 | tf_op jit(solution)/shard_map/ppermute | solution.py:573
  69.8 4.5 %collective-permute-start.2 = (bf16[64,64,128]{2,1,0:T(8,128)(2,1)}, bf16[64,64,128]{2,1,0:T(8,128)(2,1)}, u32[]{:S(2)}, u32[]{:S(2)}) collective-permute-start(bf16[64,64,128]{2,1,0:T(8,128)(2,1)} %collective-permute-done.1), channel_id=1, source_target_pairs={{16,0},{18,8},{20,16},{22,24},{24,2},{26,10},{28,18},{30,26},{0,4}... | collective-permute-start | bytes 3145736 | tf_op jit(solution)/shard_map/ppermute | solution.py:581
  74.3 0.0 copy-start.7
  74.3 0.0 copy-start.9
  74.3 2.7 copy.28.x_ref
  77.0 0.0 copy-done.2
  77.0 0.1 copy.29
  77.1 0.8 copy.32.w_ref
  77.9 0.0 copy-done.7
  77.9 0.7 copy.30.gain
  78.6 0.0 copy-done.8
  78.6 0.7 copy.31.bias
  79.3 0.0 copy-done.4
  79.3 0.0 copy-start.10
  79.3 0.8 copy.33.w_ref
  80.1 0.0 copy-done.9
  80.1 0.7 copy.34.gain
  80.8 0.9 copy.35
  81.7 0.1 add_convert_fusion
  81.8 0.0 copy-done.6
  81.8 0.6 fusion.2
  82.4 1.9 pad_add_fusion
  84.2 18.9 %backward.1 = (f32[128,64,128]{2,1,0:T(8,128)}, bf16[144,192,128]{2,1,0:T(8,128)(2,1)}) custom-call(s32[5]{0:T(128)} %get-tuple-element.73.meta, bf16[128,64,128]{2,1,0:T(8,128)(2,1)} %bitcast.41, bf16[8,64,128]{2,1,0:T(8,128)(2,1)} %get-tuple-element.45.top, bf16[8,64,128]{2,1,0:T(8,128)(2,1)} %get-tuple-element.46.bot, ...), custom_call_target="tpu_custom_call" | custom-call | tf_op jit(solution)/shard_map/backward/pallas_call | solution.py:584
  103.2 0.0 copy-done.10
  103.2 0.5 constant_dynamic-slice_fusion
  103.7 0.0 collective-permute-done.first_ref
  103.7 0.0 collective-permute-done.2.last_ref
  103.7 1.0 copy-done.1
  104.7 6.6 %sym.1 = (bf16[128,64,128]{2,1,0:T(8,128)(2,1)}, bf16[8,64,128]{2,1,0:T(8,128)(2,1)}, bf16[8,64,128]{2,1,0:T(8,128)(2,1)}, f32[64,128]{1,0:T(8,128)}) custom-call(bf16[128,64,128]{2,1,0:T(8,128)(2,1)} %copy.28.x_ref, bf16[64,64,128]{2,1,0:T(8,128)(2,1)} %copy-done.1, bf16[64,64,128]{2,1,0:T(8,128)(2,1)} %collective-permute-done.2.last_ref, ...), custom_call_target="tpu_custom_call" | custom-call | tf_op jit(solution)/shard_map/sym/pallas_call | solution.py:592
  111.3 24.3 %stats.3.stat = f32[64,128]{1,0:T(8,128)} custom-call(f32[64,128]{1,0:T(8,128)} %get-tuple-element.43.x_ref), custom_call_target="tpu_custom_call" | custom-call | tf_op jit(solution)/shard_map/stats/pallas_call | solution.py:229
  135.6 11.9 %halo.3 = (bf16[8,64,128]{2,1,0:T(8,128)(2,1)}, bf16[8,64,128]{2,1,0:T(8,128)(2,1)}, bf16[10,64,128]{2,1,0:T(8,128)(2,1)}, bf16[10,64,128]{2,1,0:T(8,128)(2,1)}) custom-call(bf16[128,64,128]{2,1,0:T(8,128)(2,1)} %get-tuple-element.36.x_ref, bf16[8,64,128]{2,1,0:T(8,128)(2,1)} %get-tuple-element.37.low_ref, bf16[8,64,128]{2,1,0:T(8,128)(2,1)} %get-tuple-element.38.high_ref), custom_call_target="tpu_custom_call" | custom-call | tf_op jit(solution)/shard_map/halo/pallas_call | solution.py:142
  147.6 29.2 %forward.1 = (f32[128,64,128]{2,1,0:T(8,128)}, bf16[144,192,128]{2,1,0:T(8,128)(2,1)}, bf16[144,192,128]{2,1,0:T(8,128)(2,1)}, f32[64,128]{1,0:T(8,128)}) custom-call(s32[5]{0:T(128)} %get-tuple-element.72.meta, s32[128]{0:T(128)} %get-tuple-element.71.ids, bf16[128,64,128]{2,1,0:T(8,128)(2,1)} %get-tuple-element.36.x_ref, ...), custom_call_target="tpu_custom_call" | custom-call | tf_op jit(solution)/shard_map/forward/pallas_call | solution.py:597
  176.8 8.6 %stats.4.stat = f32[64,128]{1,0:T(8,128)} custom-call(f32[64,128]{1,0:T(8,128)} %get-tuple-element.50.x_ref), custom_call_target="tpu_custom_call" | custom-call | tf_op jit(solution)/shard_map/stats/pallas_call | solution.py:229
  185.4 0.0 copy-start.5
  185.4 18.7 %second.1 = (f32[64,128]{1,0:T(8,128)}, f32[576,64]{1,0:T(8,128)}) custom-call(s32[5]{0:T(128)} %get-tuple-element.73.meta, f32[128,64,128]{2,1,0:T(8,128)} %get-tuple-element.44.hid_ref, f32[128,64,128]{2,1,0:T(8,128)} %get-tuple-element.49.dact_ref, f32[64,128]{1,0:T(8,128)} %stats.4.stat, f32[64,1]{1,0:T(8,128)} %copy.34.gain, ...), custom_call_target="tpu_custom_call" | custom-call | tf_op jit(solution)/shard_map/second/pallas_call | solution.py:605
  204.0 8.3 %stats.5.stat_two = f32[64,128]{1,0:T(8,128)} custom-call(f32[64,128]{1,0:T(8,128)} %get-tuple-element.52.x_ref), custom_call_target="tpu_custom_call" | custom-call | tf_op jit(solution)/shard_map/stats/pallas_call | solution.py:229
  212.3 0.0 copy-done.5
  212.4 1.0 slice_reduce_fusion.1
  213.4 0.0 copy-start.3
  213.4 25.2 %first.1 = (f32[64,128]{1,0:T(8,128)}, f32[576,64]{1,0:T(8,128)}) custom-call(s32[5]{0:T(128)} %get-tuple-element.72.meta, s32[128]{0:T(128)} %get-tuple-element.71.ids, f32[128,64,128]{2,1,0:T(8,128)} %get-tuple-element.44.hid_ref, f32[128,64,128]{2,1,0:T(8,128)} %get-tuple-element.49.dact_ref, f32[64,128]{1,0:T(8,128)} %stats.4.stat, ...), custom_call_target="tpu_custom_call" | custom-call | tf_op jit(solution)/shard_map/first/pallas_call | solution.py:613
  238.6 1.1 reshape.77
  239.7 1.0 slice_reduce_fusion.2
  240.7 0.1 reshape.79
  240.8 0.0 copy-done.3
  240.8 0.1 reshape.78
  240.9 0.8 select_maximum_fusion
  241.7 27.7 %total.1 = f32[32,24,128]{2,1,0:T(8,128)} custom-call(f32[32,24,128]{2,1,0:T(8,128)} %bitcast.45), custom_call_target="tpu_custom_call" | custom-call | tf_op jit(solution)/shard_map/total/pallas_call | solution.py:298
  269.4 1.0 fusion.1
  270.4 0.1 reshape.81
  270.5 0.9 copy.37
  271.4 0.1 reshape.82
  271.5 0.7 reverse_multiply_fusion
  272.2 0.7 slice.72
  272.9 0.1 reshape.84
  273.0 1.1 slice_reduce_fusion.3
  (8 shorter events, 0.1 us)
Async XLA Ops:
  5.0 4.0 %copy-start = (bf16[1,64,128,128]{3,2,1,0:T(8,128)(2,1)S(1)}, bf16[1,64,128,128]{3,2,1,0:T(8,128)(2,1)}, u32[]{:S(2)}) copy-start(bf16[1,64,128,128]{3,2,1,0:T(8,128)(2,1)} %param.9) | copy-start | bytes 6291460
  29.0 40.8 %collective-permute-start.1 = (bf16[64,64,128]{2,1,0:T(8,128)(2,1)S(1)}, bf16[64,64,128]{2,1,0:T(8,128)(2,1)}, u32[]{:S(2)}, u32[]{:S(2)}) collective-permute-start(bf16[64,64,128]{2,1,0:T(8,128)(2,1)S(1)} %get-tuple-element.62), channel_id=1, source_target_pairs={{0,16},{2,18},{4,20},{6,22},{8,24},{10,26},{12,28},{14,30},{16,0},... | collective-permute-start | bytes 3145736 | tf_op jit(solution)/shard_map/ppermute | solution.py:573
  30.1 73.6 %collective-permute-start = (bf16[64,64,128]{2,1,0:T(8,128)(2,1)}, bf16[64,64,128]{2,1,0:T(8,128)(2,1)S(1)}, u32[]{:S(2)}, u32[]{:S(2)}) collective-permute-start(bf16[64,64,128]{2,1,0:T(8,128)(2,1)} %get-tuple-element.63), channel_id=1, source_target_pairs={{0,0},{2,8},{4,16},{6,24},{8,2},{10,10},{12,18},{14,26},{16,4},{18... | collective-permute-start | bytes 3145736 | tf_op jit(solution)/shard_map/ppermute | solution.py:578
  69.8 33.9 %collective-permute-start.2 = (bf16[64,64,128]{2,1,0:T(8,128)(2,1)}, bf16[64,64,128]{2,1,0:T(8,128)(2,1)}, u32[]{:S(2)}, u32[]{:S(2)}) collective-permute-start(bf16[64,64,128]{2,1,0:T(8,128)(2,1)} %collective-permute-done.1), channel_id=1, source_target_pairs={{16,0},{18,8},{20,16},{22,24},{24,2},{26,10},{28,18},{30,26},{0,4}... | collective-permute-start | bytes 3145736 | tf_op jit(solution)/shard_map/ppermute | solution.py:581
  74.3 2.7 copy-start.2
  74.3 3.6 %copy-start.7 = (f32[64]{0:T(128)S(1)}, f32[64]{0:T(128)}, u32[]{:S(2)}) copy-start(f32[64]{0:T(128)} %param.15) | copy-start | bytes 772
  74.3 4.3 %copy-start.8 = (f32[64]{0:T(128)S(1)}, f32[64]{0:T(128)}, u32[]{:S(2)}) copy-start(f32[64]{0:T(128)} %param.17) | copy-start | bytes 772
  74.3 5.0 %copy-start.4 = (bf16[9,64,64]{2,1,0:T(8,128)(2,1)S(1)}, bf16[9,64,64]{2,1,0:T(8,128)(2,1)}, u32[]{:S(2)}) copy-start(bf16[9,64,64]{2,1,0:T(8,128)(2,1)} %param.14) | copy-start | bytes 221188
  74.3 5.8 %copy-start.9 = (f32[64]{0:T(128)S(1)}, f32[64]{0:T(128)}, u32[]{:S(2)}) copy-start(f32[64]{0:T(128)} %param.16) | copy-start | bytes 772
  77.0 4.8 %copy-start.6 = (s32[2]{0:T(128)S(1)}, s32[2]{0:T(128)}, u32[]{:S(2)}) copy-start(s32[2]{0:T(128)} %param.12) | copy-start | bytes 28
  79.3 23.9 %copy-start.10 = (s32[1,512]{1,0:T(1,128)S(1)}, s32[1,512]{1,0:T(1,128)}, u32[]{:S(2)}) copy-start(s32[1,512]{1,0:T(1,128)} %param.11) | copy-start | bytes 6148
  103.7 1.0 copy-start.1
  185.4 27.0 %copy-start.5 = (f32[64,128]{1,0:T(8,128)S(1)}, f32[64,128]{1,0:T(8,128)}, u32[]{:S(2)}) copy-start(f32[64,128]{1,0:T(8,128)} %get-tuple-element.43.x_ref) | copy-start | bytes 98308
  213.4 27.4 %copy-start.3 = (f32[576,64]{1,0:T(8,128)S(1)}, f32[576,64]{1,0:T(8,128)}, u32[]{:S(2)}) copy-start(f32[576,64]{1,0:T(8,128)} %get-tuple-element.56) | copy-start | bytes 442372

commit v3 on v2

--- a/solution.py
+++ b/solution.py
@@ -155,14 +155,6 @@
     )(x, low, high)
 
 
-def peer_of(index, cols, depth):
-    return {
-        "row": index // (cols * depth),
-        "col": lax.rem(index // depth, cols),
-        "dp": lax.rem(index, depth),
-    }
-
-
 def greet(barrier, me, count, peer):
     def body(step, carry):
         to = lax.rem(me + step, count)
@@ -221,6 +213,83 @@
     total = jnp.sum(slots[...], axis=0)
     filled = jnp.concatenate([total, jnp.zeros((x_ref.shape[1] - 8, chans), f32)], axis=0)
     out_ref[...] = filled.T
+
+
+def border_stats_kernel(
+    tile_ref, x_ref, low_ref, high_ref, out_ref, top_ref, bot_ref, left_ref, right_ref,
+    own, slots, send, recv, halo_send, halo_recv,
+):
+    rows, cols = lax.axis_size("row"), lax.axis_size("col")
+    count = rows * cols
+    me = lax.axis_index("row") * cols + lax.axis_index("col")
+    chans = tile_ref.shape[0]
+
+    def peer(index):
+        return {"row": index // cols, "col": lax.rem(index, cols)}
+
+    greet(pltpu.get_barrier_semaphore(), me, count, peer)
+    copies = halo_body(
+        x_ref, low_ref, high_ref, top_ref, bot_ref, left_ref, right_ref, halo_send, halo_recv
+    )
+    for copy in copies:
+        copy.start()
+    own[...] = tile_ref[...].T[0:8, :]
+
+    def copy_of(step, slot):
+        return pltpu.make_async_remote_copy(
+            src_ref=own,
+            dst_ref=slots.at[slot],
+            send_sem=send.at[step],
+            recv_sem=recv.at[slot],
+            device_id=peer(lax.rem(me + step, count)),
+            device_id_type=MESH,
+        )
+
+    def start(step, carry):
+        copy_of(step, me).start()
+        return carry
+
+    def land(step, carry):
+        copy_of(step, me).wait_send()
+        copy_of(step, lax.rem(me + step, count)).wait_recv()
+        return carry
+
+    slots[me] = own[...]
+    lax.fori_loop(1, count, start, 0)
+    lax.fori_loop(1, count, land, 0)
+    total = jnp.sum(slots[...], axis=0)
+    filled = jnp.concatenate([total, jnp.zeros((tile_ref.shape[1] - 8, chans), f32)], axis=0)
+    out_ref[...] = filled.T
+    for copy in copies:
+        copy.wait()
+
+
+def border_stats(tile, x, low, high, number):
+    side, chans, width = x.shape
+    blocks = low.shape[0]
+    count = lax.axis_size("row") * lax.axis_size("col")
+    return pl.pallas_call(
+        border_stats_kernel,
+        name="border_stats",
+        out_shape=[
+            shape(tile.shape, f32),
+            shape((reach, chans, width), bf16),
+            shape((reach, chans, width), bf16),
+            shape((blocks + 2, chans, width), bf16),
+            shape((blocks + 2, chans, width), bf16),
+        ],
+        in_specs=[vmem] + [anyspace] * 3,
+        out_specs=[vmem] + [anyspace] * 4,
+        scratch_shapes=[
+            pltpu.VMEM((8, chans), f32),
+            pltpu.VMEM((count, 8, chans), f32),
+            pltpu.SemaphoreType.DMA((count,)),
+            pltpu.SemaphoreType.DMA((count,)),
+            pltpu.SemaphoreType.DMA((8,)),
+            pltpu.SemaphoreType.DMA((8,)),
+        ],
+        compiler_params=pltpu.CompilerParams(collective_id=number, has_side_effects=True),
+    )(tile, x, low, high)
 
 
 def all_stats(tile, number):
@@ -242,36 +311,41 @@
     )(tile)
 
 
-def total_kernel(x_ref, out_ref, slots, send, recv, send_two, recv_two):
+def total_kernel(x_ref, out_ref, slots, part, col_slots, *sems):
     rows, cols, depth = lax.axis_size("row"), lax.axis_size("col"), lax.axis_size("dp")
-    count = rows * cols * depth
-    me = (lax.axis_index("row") * cols + lax.axis_index("col")) * depth + lax.axis_index("dp")
-    peer = functools.partial(peer_of, cols=cols, depth=depth)
-    greet(pltpu.get_barrier_semaphore(), me, count, peer)
-
-    def scatter(step, source):
-        to = lax.rem(me + step, count)
-        return pltpu.make_async_remote_copy(
-            src_ref=x_ref.at[to],
-            dst_ref=slots.at[source],
-            send_sem=send.at[step],
-            recv_sem=recv.at[source],
-            device_id=peer(to),
-            device_id_type=MESH,
-        )
-
-    def gather(step, source):
-        to = lax.rem(me + step, count)
-        return pltpu.make_async_remote_copy(
-            src_ref=out_ref.at[source],
-            dst_ref=out_ref.at[source],
-            send_sem=send_two.at[step],
-            recv_sem=recv_two.at[source],
-            device_id=peer(to),
-            device_id_type=MESH,
-        )
-
-    def run(make):
+    plane = rows * depth
+    mine = lax.axis_index("row") * depth + lax.axis_index("dp")
+    column = lax.axis_index("col")
+
+    def in_plane(index):
+        return {"row": index // depth, "dp": lax.rem(index, depth)}
+
+    def in_column(index):
+        return {"col": index}
+
+    barrier = pltpu.get_barrier_semaphore()
+    for me, count, peer in ((mine, plane, in_plane), (column, cols, in_column)):
+
+        def signal(step, carry, me=me, count=count, peer=peer):
+            to = peer(lax.rem(me + step, count))
+            pl.semaphore_signal(barrier, inc=1, device_id=to, device_id_type=MESH)
+            return carry
+
+        lax.fori_loop(1, count, signal, 0)
+    pl.semaphore_wait(barrier, plane + cols - 2)
+
+    def run(me, count, peer, source, target, send, recv):
+        def make(step, slot):
+            to = lax.rem(me + step, count)
+            return pltpu.make_async_remote_copy(
+                src_ref=source(to),
+                dst_ref=target(slot),
+                send_sem=send.at[step],
+                recv_sem=recv.at[slot],
+                device_id=peer(to),
+                device_id_type=MESH,
+            )
+
         def start(step, carry):
             make(step, me).start()
             return carry
@@ -284,24 +358,43 @@
         lax.fori_loop(1, count, start, 0)
         lax.fori_loop(1, count, land, 0)
 
-    slots[me] = x_ref[me]
-    run(scatter)
-    out_ref[me] = jnp.sum(slots[...], axis=0)
-    run(gather)
+    slots[mine] = x_ref[mine]
+    run(mine, plane, in_plane, lambda to: x_ref.at[to], lambda at: slots.at[at], *sems[0:2])
+    part[...] = jnp.sum(slots[...], axis=0)
+    col_slots[column] = part[column]
+    run(column, cols, in_column, lambda to: part.at[to], lambda at: col_slots.at[at], *sems[2:4])
+    out_ref[mine, column] = jnp.sum(col_slots[...], axis=0)
+    run(
+        column, cols, in_column,
+        lambda to: out_ref.at[mine, column], lambda at: out_ref.at[mine, at], *sems[4:6],
+    )
+    run(
+        mine, plane, in_plane,
+        lambda to: out_ref.at[mine], lambda at: out_ref.at[at], *sems[6:8],
+    )
 
 
 def grand_total(flat, number):
-    count = lax.axis_size("row") * lax.axis_size("col") * lax.axis_size("dp")
+    cols = lax.axis_size("col")
+    plane = lax.axis_size("row") * lax.axis_size("dp")
+    count = plane * cols
     rows = flat.shape[0]
     each = -(-rows // (8 * count)) * 8
-    padded = jnp.pad(flat, ((0, each * count - rows), (0, 0))).reshape(count, each, 128)
+    padded = jnp.pad(flat, ((0, each * count - rows), (0, 0))).reshape(plane, cols, each, 128)
     out = pl.pallas_call(
         total_kernel,
         name="total",
         out_shape=shape(padded.shape, f32),
         in_specs=[vmem],
         out_specs=vmem,
-        scratch_shapes=[pltpu.VMEM(padded.shape, f32)] + [pltpu.SemaphoreType.DMA((count,))] * 4,
+        scratch_shapes=[
+            pltpu.VMEM(padded.shape, f32),
+            pltpu.VMEM(padded.shape[1:], f32),
+            pltpu.VMEM(padded.shape[1:], f32),
+        ]
+        + [pltpu.SemaphoreType.DMA((plane,))] * 2
+        + [pltpu.SemaphoreType.DMA((cols,))] * 4
+        + [pltpu.SemaphoreType.DMA((plane,))] * 2,
         compiler_params=pltpu.CompilerParams(
             collective_id=number, has_side_effects=True, vmem_limit_bytes=LIMIT
         ),
@@ -578,9 +671,6 @@
     direct = lax.ppermute(
         turned[: side // 2], ("row", "col"), [(i * cols + j, j * cols + i) for i, j in pairs]
     )
-    onward = lax.ppermute(
-        aside, ("row", "col"), [((i ^ flip) * cols + j, j * cols + i) for i, j in pairs]
-    )
     d_act, cot_stack = compute(
         functools.partial(backward_kernel, length=length),
         "backward",
@@ -588,12 +678,15 @@
         [smem] + [vmem] * 6,
         [centre, border, border],
     )(meta_two, cot, top, bot, left, right, backward_w)
+    aside, d_act = lax.optimization_barrier((aside, d_act))
+    onward = lax.ppermute(
+        aside, ("row", "col"), [((i ^ flip) * cols + j, j * cols + i) for i, j in pairs]
+    )
 
     sym, low, high, stat_one = compute(
         sym_kernel, "sym", [shape(full, bf16), edge, edge, stats], [vmem] * 4
     )(tile, direct, onward, cot)
-    top, bot, left, right = halo(sym, low, high, 2)
-    all_one = all_stats(stat_one, 3)
+    all_one, top, bot, left, right = border_stats(stat_one, sym, low, high, 2)
     hid, act_stack, slope_stack, stat_two = compute(
         functools.partial(forward_kernel, count=count),
         "forward",

time: 275 us -> 266 us (0.967)
  waiting for transfers between devices: 37.8 us -> 31.8 us
  Pallas kernels: 198 us -> 195 us
    pallas_call x0 -> x1, Pallas kernels: none -> 39.2 us  [border_stats(): pl.pallas_call(border_stats_kernel, name='border_stats', out_shape=[shape...]
    pallas_call x3 -> x2, Pallas kernels: 41.2 us -> 16.5 us  [all_stats(): pl.pallas_call(stats_kernel, name='stats', out_shape=shape(tile.shape, f3...]
    ppermute x1, waiting for transfers between devices: 37.8 us -> 16.1 us  [local(): lax.ppermute(turned[side // 2:], ('row', 'col'), [(i * cols + j, (i ^ fli...]
    ppermute x1, waiting for transfers between devices: 0.01 us -> 15.8 us  [local(): lax.ppermute(aside, ('row', 'col'), [((i ^ flip) * cols + j, j * cols + i...]
    pallas_call x2 -> x1, Pallas kernels: 26.4 us -> 14.4 us  [halo(): pl.pallas_call(halo_kernel, name='halo', out_shape=[shape((reach, chans,...]
    pallas_call x1, Pallas kernels: 27.7 us -> 22.6 us  [grand_total(): pl.pallas_call(total_kernel, name='total', out_shape=shape(padded.shape,...]
  transfers between devices with their start and end apart: 3 -> 3, of which waited for: 1 -> 2; matrix products, arithmetic and copies ran while one was open for 4% -> 4% of each run, Pallas kernels for 7% -> 7%
where the time goes in v3:
time: 266 us; the launch traced here: 265 us
  Pallas kernels  195 us (73%)
  waiting for transfers between devices  31.8 us (12%)
  local copies, waits for them, and re-layouts  23.9 us (9%)
  starting transfers between devices  7.36 us (3%)
  other arithmetic  5.65 us (2%)
    pallas_call x1, Pallas kernels, border_stats(): pl.pallas_call(border_stats_kernel, name='border_stats', out_shape=[shape...  39.2 us
    pallas_call x1, Pallas kernels, local(): compute(functools.partial(forward_kernel, count=count), 'forward', [shape...  29.2 us
    pallas_call x1, Pallas kernels, local(): compute(functools.partial(first_kernel, count=count), 'first', [stats, sh...  25.2 us
    pallas_call x1, Pallas kernels, grand_total(): pl.pallas_call(total_kernel, name='total', out_shape=shape(padded.shape,...  22.6 us
    pallas_call x1, Pallas kernels, local(): compute(functools.partial(backward_kernel, length=length), 'backward', [s...  18.9 us
    pallas_call x1, Pallas kernels, local(): compute(functools.partial(second_kernel, count=count), 'second', [stats,...  18.7 us
    pallas_call x2, Pallas kernels, all_stats(): pl.pallas_call(stats_kernel, name='stats', out_shape=shape(tile.shape, f3...  16.5 us
    ppermute x1, waiting for transfers between devices, local(): lax.ppermute(turned[side // 2:], ('row', 'col'), [(i * cols + j, (i ^ fli...  16.1 us
  transfers between devices with their start and end apart: 3, of which 2 were waited for; matrix products, arithmetic and copies ran while one was open for 4% of the time, Pallas kernels for 7%

profile of v3, /device:TPU:0, one launch (start us, length us, event | category | flops | bytes accessed | tf_op | source)
XLA Modules:
  0.0 265.0 jit_solution(12107660257320175061)
XLA Ops:
  0.6 4.3 %copy.40 = bf16[1,64,128,128]{3,1,2,0:T(8,128)(2,1)} copy(bf16[1,64,128,128]{3,2,1,0:T(8,128)(2,1)} %param.10) | data formatting | bytes 4194304 | tf_op args[1]
  5.0 0.0 copy-start
  5.0 4.0 %edges.1 = (bf16[8,64,128]{2,1,0:T(8,128)(2,1)}, bf16[8,64,128]{2,1,0:T(8,128)(2,1)}) custom-call(bf16[128,64,128]{2,1,0:T(8,128)(2,1)} %bitcast.43), custom_call_target="tpu_custom_call" | custom-call | tf_op jit(solution)/shard_map/edges/pallas_call | solution.py:660
  9.0 0.0 copy-done
  9.0 2.9 %copy.26 = bf16[1,64,128,128]{2,1,3,0:T(8,128)(2,1)} copy(bf16[1,64,128,128]{3,2,1,0:T(8,128)(2,1)S(1)} %copy-done) | data formatting | bytes 4194304 | tf_op args[0]
  11.9 14.4 %halo.1 = (bf16[8,64,128]{2,1,0:T(8,128)(2,1)}, bf16[8,64,128]{2,1,0:T(8,128)(2,1)}, bf16[10,64,128]{2,1,0:T(8,128)(2,1)}, bf16[10,64,128]{2,1,0:T(8,128)(2,1)}) custom-call(bf16[128,64,128]{2,1,0:T(8,128)(2,1)} %bitcast.44, bf16[8,64,128]{2,1,0:T(8,128)(2,1)} %get-tuple-element.35.low_ref, bf16[8,64,128]{2,1,0:T(8,128)(2,1)} %get-tuple-element.36.high_ref), custom_call_target="tpu_custom_call" | custom-call | tf_op jit(solution)/shard_map/halo/pallas_call | solution.py:142
  26.3 0.0 copy-start.4
  26.3 0.0 copy-start.6
  26.3 3.1 %fusion = (bf16[64,64,128]{2,1,0:T(8,128)(2,1)}, bf16[64,64,128]{2,1,0:T(8,128)(2,1)}) fusion(bf16[128,64,128]{2,1,0:T(8,128)(2,1)} %bitcast.48), kind=kLoop, calls=%fused_computation.20 | loop fusion | bytes 4194304 | tf_op jit(solution)/shard_map/slice | solution.py:667
  29.4 1.1 collective-permute-start.1
  30.5 1.9 collective-permute-start
  32.4 0.0 copy-done.4
  32.4 0.8 copy.28.w_ref
  33.2 0.1 add_convert_fusion
  33.2 0.0 copy-done.6
  33.2 0.6 fusion.2
  33.8 1.9 pad_add_fusion
  35.7 18.9 %backward.1 = (f32[128,64,128]{2,1,0:T(8,128)}, bf16[144,192,128]{2,1,0:T(8,128)(2,1)}) custom-call(s32[5]{0:T(128)} %get-tuple-element.79.meta, bf16[128,64,128]{2,1,0:T(8,128)(2,1)} %bitcast.45, bf16[8,64,128]{2,1,0:T(8,128)(2,1)} %get-tuple-element.39.top, bf16[8,64,128]{2,1,0:T(8,128)(2,1)} %get-tuple-element.40.bot, ...), custom_call_target="tpu_custom_call" | custom-call | tf_op jit(solution)/shard_map/backward/pallas_call | solution.py:674
  54.6 16.1 %collective-permute-done.1 = bf16[64,64,128]{2,1,0:T(8,128)(2,1)} collective-permute-done((bf16[64,64,128]{2,1,0:T(8,128)(2,1)}, bf16[64,64,128]{2,1,0:T(8,128)(2,1)}, u32[]{:S(2)}, u32[]{:S(2)}) %collective-permute-start.1) | collective-permute-done | bytes 1048608 | tf_op jit(solution)/shard_map/ppermute | solution.py:666
  70.7 4.4 %collective-permute-start.2 = (bf16[64,64,128]{2,1,0:T(8,128)(2,1)}, bf16[64,64,128]{2,1,0:T(8,128)(2,1)}, u32[]{:S(2)}, u32[]{:S(2)}) collective-permute-start(bf16[64,64,128]{2,1,0:T(8,128)(2,1)} %collective-permute-done.1), channel_id=1, source_target_pairs={{16,0},{18,8},{20,16},{22,24},{24,2},{26,10},{28,18},{30,26},{0,4}... | collective-permute-start | bytes 3145736 | tf_op jit(solution)/shard_map/ppermute | solution.py:682
  75.1 0.0 copy-start.2
  75.1 0.0 copy-start.10
  75.1 2.7 %copy.29.x_ref = bf16[128,64,128]{2,1,0:T(8,128)(2,1)} copy(bf16[128,64,128]{2,0,1:T(8,128)(2,1)S(1)} %bitcast.47) | data formatting | bytes 4194304 | tf_op jit(solution)/shard_map/transpose | solution.py:641
  77.8 0.0 copy-done.2
  77.8 0.1 copy.30
  78.0 0.8 copy.33.w_ref
  78.8 0.0 copy-done.7
  78.8 0.7 copy.31.gain
  79.5 0.0 copy-done.8
  79.5 0.7 copy.32.bias
  80.2 0.0 copy-done.9
  80.2 0.7 copy.34.gain
  80.9 0.9 copy.35
  81.8 0.0 copy-done.10
  81.8 0.5 constant_dynamic-slice_fusion
  82.3 0.0 collective-permute-done.first_ref
  82.3 15.8 %collective-permute-done.2.last_ref = bf16[64,64,128]{2,1,0:T(8,128)(2,1)} collective-permute-done((bf16[64,64,128]{2,1,0:T(8,128)(2,1)}, bf16[64,64,128]{2,1,0:T(8,128)(2,1)}, u32[]{:S(2)}, u32[]{:S(2)}) %collective-permute-start.2) | collective-permute-done | bytes 1048608 | tf_op jit(solution)/shard_map/ppermute | solution.py:682
  98.0 0.0 copy-done.1
  98.0 6.6 %sym.1 = (bf16[128,64,128]{2,1,0:T(8,128)(2,1)}, bf16[8,64,128]{2,1,0:T(8,128)(2,1)}, bf16[8,64,128]{2,1,0:T(8,128)(2,1)}, f32[64,128]{1,0:T(8,128)}) custom-call(bf16[128,64,128]{2,1,0:T(8,128)(2,1)} %copy.29.x_ref, bf16[64,64,128]{2,1,0:T(8,128)(2,1)} %copy-done.1, bf16[64,64,128]{2,1,0:T(8,128)(2,1)} %collective-permute-done.2.last_ref, ...), custom_call_target="tpu_custom_call" | custom-call | tf_op jit(solution)/shard_map/sym/pallas_call | solution.py:686
  104.7 39.2 %border_stats.1 = (f32[64,128]{1,0:T(8,128)}, bf16[8,64,128]{2,1,0:T(8,128)(2,1)}, bf16[8,64,128]{2,1,0:T(8,128)(2,1)}, bf16[10,64,128]{2,1,0:T(8,128)(2,1)}, bf16[10,64,128]{2,1,0:T(8,128)(2,1)}) custom-call(f32[64,128]{1,0:T(8,128)} %get-tuple-element.46.tile_ref, bf16[128,64,128]{2,1,0:T(8,128)(2,1)} %get-tuple-element.45.x_ref, ...), custom_call_target="tpu_custom_call" | custom-call | tf_op jit(solution)/shard_map/border_stats/pallas_call | solution.py:271
  143.9 29.2 %forward.1 = (f32[128,64,128]{2,1,0:T(8,128)}, bf16[144,192,128]{2,1,0:T(8,128)(2,1)}, bf16[144,192,128]{2,1,0:T(8,128)(2,1)}, f32[64,128]{1,0:T(8,128)}) custom-call(s32[5]{0:T(128)} %get-tuple-element.78.meta, s32[128]{0:T(128)} %get-tuple-element.77.ids, bf16[128,64,128]{2,1,0:T(8,128)(2,1)} %get-tuple-element.45.x_ref, ...), custom_call_target="tpu_custom_call" | custom-call | tf_op jit(solution)/shard_map/forward/pallas_call | solution.py:690
  173.1 8.3 %stats.2.stat = f32[64,128]{1,0:T(8,128)} custom-call(f32[64,128]{1,0:T(8,128)} %get-tuple-element.56.x_ref), custom_call_target="tpu_custom_call" | custom-call | tf_op jit(solution)/shard_map/stats/pallas_call | solution.py:298
  181.4 0.0 copy-start.5
  181.4 18.7 %second.1 = (f32[64,128]{1,0:T(8,128)}, f32[576,64]{1,0:T(8,128)}) custom-call(s32[5]{0:T(128)} %get-tuple-element.79.meta, f32[128,64,128]{2,1,0:T(8,128)} %get-tuple-element.54.hid_ref, f32[128,64,128]{2,1,0:T(8,128)} %get-tuple-element.55.dact_ref, f32[64,128]{1,0:T(8,128)} %stats.2.stat, f32[64,1]{1,0:T(8,128)} %copy.34.gain, ...), custom_call_target="tpu_custom_call" | custom-call | tf_op jit(solution)/shard_map/second/pallas_call | solution.py:698
  200.1 8.3 %stats.3.stat_two = f32[64,128]{1,0:T(8,128)} custom-call(f32[64,128]{1,0:T(8,128)} %get-tuple-element.58.x_ref), custom_call_target="tpu_custom_call" | custom-call | tf_op jit(solution)/shard_map/stats/pallas_call | solution.py:298
  208.4 0.0 copy-done.5
  208.4 1.0 slice_reduce_fusion.1
  209.4 0.0 copy-start.3
  209.4 25.2 %first.1 = (f32[64,128]{1,0:T(8,128)}, f32[576,64]{1,0:T(8,128)}) custom-call(s32[5]{0:T(128)} %get-tuple-element.78.meta, s32[128]{0:T(128)} %get-tuple-element.77.ids, f32[128,64,128]{2,1,0:T(8,128)} %get-tuple-element.54.hid_ref, f32[128,64,128]{2,1,0:T(8,128)} %get-tuple-element.55.dact_ref, f32[64,128]{1,0:T(8,128)} %stats.2.stat, ...), custom_call_target="tpu_custom_call" | custom-call | tf_op jit(solution)/shard_map/first/pallas_call | solution.py:706
  234.6 1.1 reshape.77
  235.7 1.0 slice_reduce_fusion.2
  236.7 0.1 reshape.79
  236.8 0.0 copy-done.3
  236.8 0.1 reshape.78
  236.9 0.8 select_maximum_fusion
  237.7 22.6 %total.1 = f32[8,4,24,128]{3,2,1,0:T(8,128)} custom-call(f32[8,4,24,128]{3,2,1,0:T(8,128)} %bitcast.49), custom_call_target="tpu_custom_call" | custom-call | tf_op jit(solution)/shard_map/total/pallas_call | solution.py:384
  260.3 1.0 fusion.1
  261.3 0.1 reshape.81
  261.4 0.9 copy.37
  262.3 0.1 reshape.82
  262.4 0.7 reverse_multiply_fusion
  263.1 0.7 slice.72
  263.8 0.1 reshape.84
  263.9 1.1 slice_reduce_fusion.3
  (7 shorter events, 0.1 us)
Async XLA Ops:
  5.0 4.0 %copy-start = (bf16[1,64,128,128]{3,2,1,0:T(8,128)(2,1)S(1)}, bf16[1,64,128,128]{3,2,1,0:T(8,128)(2,1)}, u32[]{:S(2)}) copy-start(bf16[1,64,128,128]{3,2,1,0:T(8,128)(2,1)} %param.9) | copy-start | bytes 6291460
  26.3 6.1 %copy-start.4 = (bf16[9,64,64]{2,1,0:T(8,128)(2,1)S(1)}, bf16[9,64,64]{2,1,0:T(8,128)(2,1)}, u32[]{:S(2)}) copy-start(bf16[9,64,64]{2,1,0:T(8,128)(2,1)} %param.14) | copy-start | bytes 221188
  26.3 6.9 %copy-start.6 = (s32[2]{0:T(128)S(1)}, s32[2]{0:T(128)}, u32[]{:S(2)}) copy-start(s32[2]{0:T(128)} %param.12) | copy-start | bytes 28
  29.4 41.3 %collective-permute-start.1 = (bf16[64,64,128]{2,1,0:T(8,128)(2,1)}, bf16[64,64,128]{2,1,0:T(8,128)(2,1)}, u32[]{:S(2)}, u32[]{:S(2)}) collective-permute-start(bf16[64,64,128]{2,1,0:T(8,128)(2,1)} %get-tuple-element.68), channel_id=1, source_target_pairs={{0,16},{2,18},{4,20},{6,22},{8,24},{10,26},{12,28},{14,30},{16,0},... | collective-permute-start | bytes 3145736 | tf_op jit(solution)/shard_map/ppermute | solution.py:666
  30.5 51.8 %collective-permute-start = (bf16[64,64,128]{2,1,0:T(8,128)(2,1)}, bf16[64,64,128]{2,1,0:T(8,128)(2,1)S(1)}, u32[]{:S(2)}, u32[]{:S(2)}) collective-permute-start(bf16[64,64,128]{2,1,0:T(8,128)(2,1)} %get-tuple-element.69), channel_id=1, source_target_pairs={{0,0},{2,8},{4,16},{6,24},{8,2},{10,10},{12,18},{14,26},{16,4},{18... | collective-permute-start | bytes 3145736 | tf_op jit(solution)/shard_map/ppermute | solution.py:671
  70.7 27.3 %collective-permute-start.2 = (bf16[64,64,128]{2,1,0:T(8,128)(2,1)}, bf16[64,64,128]{2,1,0:T(8,128)(2,1)}, u32[]{:S(2)}, u32[]{:S(2)}) collective-permute-start(bf16[64,64,128]{2,1,0:T(8,128)(2,1)} %collective-permute-done.1), channel_id=1, source_target_pairs={{16,0},{18,8},{20,16},{22,24},{24,2},{26,10},{28,18},{30,26},{0,4}... | collective-permute-start | bytes 3145736 | tf_op jit(solution)/shard_map/ppermute | solution.py:682
  75.1 2.8 %copy-start.2 = (bf16[9,64,64]{2,1,0:T(8,128)(2,1)S(1)}, bf16[9,64,64]{2,1,0:T(8,128)(2,1)}, u32[]{:S(2)}) copy-start(bf16[9,64,64]{2,1,0:T(8,128)(2,1)} %param.13) | copy-start | bytes 221188
  75.1 3.7 %copy-start.7 = (f32[64]{0:T(128)S(1)}, f32[64]{0:T(128)}, u32[]{:S(2)}) copy-start(f32[64]{0:T(128)} %param.15) | copy-start | bytes 772
  75.1 4.4 %copy-start.8 = (f32[64]{0:T(128)S(1)}, f32[64]{0:T(128)}, u32[]{:S(2)}) copy-start(f32[64]{0:T(128)} %param.17) | copy-start | bytes 772
  75.1 5.1 %copy-start.9 = (f32[64]{0:T(128)S(1)}, f32[64]{0:T(128)}, u32[]{:S(2)}) copy-start(f32[64]{0:T(128)} %param.16) | copy-start | bytes 772
  75.1 6.7 %copy-start.10 = (s32[1,512]{1,0:T(1,128)S(1)}, s32[1,512]{1,0:T(1,128)}, u32[]{:S(2)}) copy-start(s32[1,512]{1,0:T(1,128)} %param.11) | copy-start | bytes 6148
  82.3 15.8 %copy-start.1 = (bf16[64,64,128]{2,1,0:T(8,128)(2,1)}, bf16[64,64,128]{2,1,0:T(8,128)(2,1)S(1)}, u32[]{:S(2)}) copy-start(bf16[64,64,128]{2,1,0:T(8,128)(2,1)S(1)} %collective-permute-done.first_ref) | copy-start | bytes 3145732
  181.4 27.0 %copy-start.5 = (f32[64,128]{1,0:T(8,128)S(1)}, f32[64,128]{1,0:T(8,128)}, u32[]{:S(2)}) copy-start(f32[64,128]{1,0:T(8,128)} %get-tuple-element.46.tile_ref) | copy-start | bytes 98308
  209.4 27.4 %copy-start.3 = (f32[576,64]{1,0:T(8,128)S(1)}, f32[576,64]{1,0:T(8,128)}, u32[]{:S(2)}) copy-start(f32[576,64]{1,0:T(8,128)} %get-tuple-element.62) | copy-start | bytes 442372

commit v4 on v3

--- a/solution.py
+++ b/solution.py
@@ -8,6 +8,7 @@
 from jax.sharding import PartitionSpec as P
 
 reach = 8
+group = 8
 eps = 1e-05
 f32 = jnp.float32
 bf16 = jnp.bfloat16
@@ -450,13 +451,13 @@
     stack_shifts(centre, low, high, stack_ref, dil)
 
     def body(step, carry):
-        p = 4 * step
-        got = jnp.dot(w_ref[...], taps_of(stack_ref, p, dil, 4), preferred_element_type=f32)
-        for k in range(4):
+        p = group * step
+        got = jnp.dot(w_ref[...], taps_of(stack_ref, p, dil, group), preferred_element_type=f32)
+        for k in range(group):
             out_ref[p + k] = got[:, side * k : side * (k + 1)] * (1.0 / length)
         return carry
 
-    lax.fori_loop(0, side // 4, body, 0)
+    lax.fori_loop(0, side // group, body, 0)
 
 
 def moments(stat, count):
@@ -514,9 +515,9 @@
 
     def body(step, carry):
         one, two = carry
-        p = 4 * step
-        got = jnp.dot(w_ref[...], taps_of(act_ref, p, dil, 4), preferred_element_type=f32)
-        for k in range(4):
+        p = group * step
+        got = jnp.dot(w_ref[...], taps_of(act_ref, p, dil, group), preferred_element_type=f32)
+        for k in range(group):
             hid = got[:, side * k : side * (k + 1)] + jnp.where(cols != ids[p + k], biased, 0.0)
             hid_ref[p + k] = hid
             one = one + hid
@@ -524,7 +525,7 @@
         return one, two
 
     zero = jnp.zeros((chans, side), f32)
-    sums_ref[...] = as_columns(lax.fori_loop(0, side // 4, body, (zero, zero)), chans, side)
+    sums_ref[...] = as_columns(lax.fori_loop(0, side // group, body, (zero, zero)), chans, side)
 
 
 def second_kernel(
@@ -540,9 +541,9 @@
 
     def body(step, carry):
         sums = list(carry)
-        p = 4 * step
+        p = group * step
         acts = []
-        for k in range(4):
+        for k in range(group):
             dact = dact_ref[p + k]
             norm = (hid_ref[p + k] - mean) * scale
             z = gained * norm
@@ -556,7 +557,7 @@
             sums[2] = sums[2] + dz * norm
             sums[3] = sums[3] + act.astype(f32) * dact
         grad_ref[...] += lax.dot_general(
-            taps_of(stack_ref, p, dil, 4),
+            taps_of(stack_ref, p, dil, group),
             jnp.concatenate(acts, axis=1),
             (((1,), (1,)), ((), ())),
             preferred_element_type=f32,
@@ -564,7 +565,7 @@
         return tuple(sums)
 
     zero = jnp.zeros((chans, side), f32)
-    sums = lax.fori_loop(0, side // 4, body, (zero,) * 4)
+    sums = lax.fori_loop(0, side // group, body, (zero,) * 4)
     sums_ref[...] = as_columns(sums, chans, side)
 
 
@@ -585,9 +586,9 @@
     slope_grad[...] = jnp.zeros_like(slope_grad)
 
     def body(step, total):
-        p = 4 * step
+        p = group * step
         lows = []
-        for k in range(4):
+        for k in range(group):
             norm = (hid_ref[p + k] - mean) * scale
             z = gained * norm
             slope = jnp.where(z > 0, 1.0, jnp.exp(jnp.minimum(z, 0.0)))
@@ -598,14 +599,14 @@
         low = jnp.concatenate(lows, axis=1)
         dims = (((1,), (1,)), ((), ()))
         grad_ref[...] += lax.dot_general(
-            taps_of(act_ref, p, dil, 4), low, dims, preferred_element_type=f32
+            taps_of(act_ref, p, dil, group), low, dims, preferred_element_type=f32
         )
         slope_grad[...] += lax.dot_general(
-            taps_of(slope_ref, p, dil, 4), low, dims, preferred_element_type=f32
+            taps_of(slope_ref, p, dil, group), low, dims, preferred_element_type=f32
         )
         return total
 
-    total = lax.fori_loop(0, side // 4, body, jnp.zeros((chans, side), f32))
+    total = lax.fori_loop(0, side // group, body, jnp.zeros((chans, side), f32))
     gain_grad = jnp.zeros((chans, chans), f32)
     for t in range(9):
         part = pl.ds(t * chans, chans)

time: 266 us -> 257 us (0.966)
  Pallas kernels: 195 us -> 184 us
    pallas_call x1, Pallas kernels: 18.7 us -> 15.2 us  [local(): compute(functools.partial(second_kernel, count=count), 'second', [stats,...]
    pallas_call x1, Pallas kernels: 25.2 us -> 22.1 us  [local(): compute(functools.partial(first_kernel, count=count), 'first', [stats, sh...]
where the time goes in v4:
time: 257 us; the launch traced here: 256 us
  Pallas kernels  184 us (72%)
  waiting for transfers between devices  33.9 us (13%)
  local copies, waits for them, and re-layouts  23.9 us (9%)
  starting transfers between devices  7.36 us (3%)
  other arithmetic  5.65 us (2%)
    pallas_call x1, Pallas kernels, border_stats(): pl.pallas_call(border_stats_kernel, name='border_stats', out_shape=[shape...  39.2 us
    pallas_call x1, Pallas kernels, local(): compute(functools.partial(forward_kernel, count=count), 'forward', [shape...  26.8 us
    pallas_call x1, Pallas kernels, grand_total(): pl.pallas_call(total_kernel, name='total', out_shape=shape(padded.shape,...  22.6 us
    pallas_call x1, Pallas kernels, local(): compute(functools.partial(first_kernel, count=count), 'first', [stats, sh...  22.1 us
    ppermute x1, waiting for transfers between devices, local(): lax.ppermute(turned[side // 2:], ('row', 'col'), [(i * cols + j, (i ^ fli...  18.1 us
    pallas_call x1, Pallas kernels, local(): compute(functools.partial(backward_kernel, length=length), 'backward', [s...  16.9 us
    pallas_call x2, Pallas kernels, all_stats(): pl.pallas_call(stats_kernel, name='stats', out_shape=shape(tile.shape, f3...  16.5 us
    ppermute x1, waiting for transfers between devices, local(): lax.ppermute(aside, ('row', 'col'), [((i ^ flip) * cols + j, j * cols + i...  15.8 us
  transfers between devices with their start and end apart: 3, of which 2 were waited for; matrix products, arithmetic and copies ran while one was open for 4% of the time, Pallas kernels for 7%

profile of v4, /device:TPU:0, one launch (start us, length us, event | category | flops | bytes accessed | tf_op | source)
XLA Modules:
  0.0 256.0 jit_solution(11096407154036908010)
XLA Ops:
  0.6 4.3 %copy.40 = bf16[1,64,128,128]{3,1,2,0:T(8,128)(2,1)} copy(bf16[1,64,128,128]{3,2,1,0:T(8,128)(2,1)} %param.10) | data formatting | bytes 4194304 | tf_op args[1]
  5.0 0.0 copy-start
  5.0 4.0 %edges.1 = (bf16[8,64,128]{2,1,0:T(8,128)(2,1)}, bf16[8,64,128]{2,1,0:T(8,128)(2,1)}) custom-call(bf16[128,64,128]{2,1,0:T(8,128)(2,1)} %bitcast.43), custom_call_target="tpu_custom_call" | custom-call | tf_op jit(solution)/shard_map/edges/pallas_call | solution.py:661
  9.0 0.0 copy-done
  9.0 2.9 %copy.26 = bf16[1,64,128,128]{2,1,3,0:T(8,128)(2,1)} copy(bf16[1,64,128,128]{3,2,1,0:T(8,128)(2,1)S(1)} %copy-done) | data formatting | bytes 4194304 | tf_op args[0]
  11.9 14.4 %halo.1 = (bf16[8,64,128]{2,1,0:T(8,128)(2,1)}, bf16[8,64,128]{2,1,0:T(8,128)(2,1)}, bf16[10,64,128]{2,1,0:T(8,128)(2,1)}, bf16[10,64,128]{2,1,0:T(8,128)(2,1)}) custom-call(bf16[128,64,128]{2,1,0:T(8,128)(2,1)} %bitcast.44, bf16[8,64,128]{2,1,0:T(8,128)(2,1)} %get-tuple-element.35.low_ref, bf16[8,64,128]{2,1,0:T(8,128)(2,1)} %get-tuple-element.36.high_ref), custom_call_target="tpu_custom_call" | custom-call | tf_op jit(solution)/shard_map/halo/pallas_call | solution.py:143
  26.3 0.0 copy-start.4
  26.3 0.0 copy-start.6
  26.3 3.1 %fusion = (bf16[64,64,128]{2,1,0:T(8,128)(2,1)}, bf16[64,64,128]{2,1,0:T(8,128)(2,1)}) fusion(bf16[128,64,128]{2,1,0:T(8,128)(2,1)} %bitcast.48), kind=kLoop, calls=%fused_computation.20 | loop fusion | bytes 4194304 | tf_op jit(solution)/shard_map/slice | solution.py:668
  29.4 1.1 collective-permute-start.1
  30.5 1.9 collective-permute-start
  32.4 0.0 copy-done.4
  32.4 0.8 copy.28.w_ref
  33.2 0.1 add_convert_fusion
  33.2 0.0 copy-done.6
  33.2 0.6 fusion.2
  33.8 1.9 pad_add_fusion
  35.7 16.9 %backward.1 = (f32[128,64,128]{2,1,0:T(8,128)}, bf16[144,192,128]{2,1,0:T(8,128)(2,1)}) custom-call(s32[5]{0:T(128)} %get-tuple-element.79.meta, bf16[128,64,128]{2,1,0:T(8,128)(2,1)} %bitcast.45, bf16[8,64,128]{2,1,0:T(8,128)(2,1)} %get-tuple-element.39.top, bf16[8,64,128]{2,1,0:T(8,128)(2,1)} %get-tuple-element.40.bot, ...), custom_call_target="tpu_custom_call" | custom-call | tf_op jit(solution)/shard_map/backward/pallas_call | solution.py:675
  52.6 18.1 %collective-permute-done.1 = bf16[64,64,128]{2,1,0:T(8,128)(2,1)} collective-permute-done((bf16[64,64,128]{2,1,0:T(8,128)(2,1)}, bf16[64,64,128]{2,1,0:T(8,128)(2,1)}, u32[]{:S(2)}, u32[]{:S(2)}) %collective-permute-start.1) | collective-permute-done | bytes 1048608 | tf_op jit(solution)/shard_map/ppermute | solution.py:667
  70.7 4.4 %collective-permute-start.2 = (bf16[64,64,128]{2,1,0:T(8,128)(2,1)}, bf16[64,64,128]{2,1,0:T(8,128)(2,1)}, u32[]{:S(2)}, u32[]{:S(2)}) collective-permute-start(bf16[64,64,128]{2,1,0:T(8,128)(2,1)} %collective-permute-done.1), channel_id=1, source_target_pairs={{16,0},{18,8},{20,16},{22,24},{24,2},{26,10},{28,18},{30,26},{0,4}... | collective-permute-start | bytes 3145736 | tf_op jit(solution)/shard_map/ppermute | solution.py:683
  75.1 0.0 copy-start.2
  75.1 0.0 copy-start.10
  75.1 2.7 %copy.29.x_ref = bf16[128,64,128]{2,1,0:T(8,128)(2,1)} copy(bf16[128,64,128]{2,0,1:T(8,128)(2,1)S(1)} %bitcast.47) | data formatting | bytes 4194304 | tf_op jit(solution)/shard_map/transpose | solution.py:642
  77.8 0.0 copy-done.2
  77.8 0.1 copy.30
  78.0 0.8 copy.33.w_ref
  78.8 0.0 copy-done.7
  78.8 0.7 copy.31.gain
  79.5 0.0 copy-done.8
  79.5 0.7 copy.32.bias
  80.2 0.0 copy-done.9
  80.2 0.7 copy.34.gain
  80.9 0.9 copy.35
  81.8 0.0 copy-done.10
  81.8 0.5 constant_dynamic-slice_fusion
  82.3 0.0 collective-permute-done.first_ref
  82.3 15.8 %collective-permute-done.2.last_ref = bf16[64,64,128]{2,1,0:T(8,128)(2,1)} collective-permute-done((bf16[64,64,128]{2,1,0:T(8,128)(2,1)}, bf16[64,64,128]{2,1,0:T(8,128)(2,1)}, u32[]{:S(2)}, u32[]{:S(2)}) %collective-permute-start.2) | collective-permute-done | bytes 1048608 | tf_op jit(solution)/shard_map/ppermute | solution.py:683
  98.0 0.0 copy-done.1
  98.0 6.6 %sym.1 = (bf16[128,64,128]{2,1,0:T(8,128)(2,1)}, bf16[8,64,128]{2,1,0:T(8,128)(2,1)}, bf16[8,64,128]{2,1,0:T(8,128)(2,1)}, f32[64,128]{1,0:T(8,128)}) custom-call(bf16[128,64,128]{2,1,0:T(8,128)(2,1)} %copy.29.x_ref, bf16[64,64,128]{2,1,0:T(8,128)(2,1)} %copy-done.1, bf16[64,64,128]{2,1,0:T(8,128)(2,1)} %collective-permute-done.2.last_ref, ...), custom_call_target="tpu_custom_call" | custom-call | tf_op jit(solution)/shard_map/sym/pallas_call | solution.py:687
  104.7 39.2 %border_stats.1 = (f32[64,128]{1,0:T(8,128)}, bf16[8,64,128]{2,1,0:T(8,128)(2,1)}, bf16[8,64,128]{2,1,0:T(8,128)(2,1)}, bf16[10,64,128]{2,1,0:T(8,128)(2,1)}, bf16[10,64,128]{2,1,0:T(8,128)(2,1)}) custom-call(f32[64,128]{1,0:T(8,128)} %get-tuple-element.46.tile_ref, bf16[128,64,128]{2,1,0:T(8,128)(2,1)} %get-tuple-element.45.x_ref, ...), custom_call_target="tpu_custom_call" | custom-call | tf_op jit(solution)/shard_map/border_stats/pallas_call | solution.py:272
  143.9 26.8 %forward.1 = (f32[128,64,128]{2,1,0:T(8,128)}, bf16[144,192,128]{2,1,0:T(8,128)(2,1)}, bf16[144,192,128]{2,1,0:T(8,128)(2,1)}, f32[64,128]{1,0:T(8,128)}) custom-call(s32[5]{0:T(128)} %get-tuple-element.78.meta, s32[128]{0:T(128)} %get-tuple-element.77.ids, bf16[128,64,128]{2,1,0:T(8,128)(2,1)} %get-tuple-element.45.x_ref, ...), custom_call_target="tpu_custom_call" | custom-call | tf_op jit(solution)/shard_map/forward/pallas_call | solution.py:691
  170.8 8.3 %stats.2.stat = f32[64,128]{1,0:T(8,128)} custom-call(f32[64,128]{1,0:T(8,128)} %get-tuple-element.56.x_ref), custom_call_target="tpu_custom_call" | custom-call | tf_op jit(solution)/shard_map/stats/pallas_call | solution.py:299
  179.0 0.0 copy-start.5
  179.0 15.2 %second.1 = (f32[64,128]{1,0:T(8,128)}, f32[576,64]{1,0:T(8,128)}) custom-call(s32[5]{0:T(128)} %get-tuple-element.79.meta, f32[128,64,128]{2,1,0:T(8,128)} %get-tuple-element.54.hid_ref, f32[128,64,128]{2,1,0:T(8,128)} %get-tuple-element.55.dact_ref, f32[64,128]{1,0:T(8,128)} %stats.2.stat, f32[64,1]{1,0:T(8,128)} %copy.34.gain, ...), custom_call_target="tpu_custom_call" | custom-call | tf_op jit(solution)/shard_map/second/pallas_call | solution.py:699
  194.2 8.3 %stats.3.stat_two = f32[64,128]{1,0:T(8,128)} custom-call(f32[64,128]{1,0:T(8,128)} %get-tuple-element.58.x_ref), custom_call_target="tpu_custom_call" | custom-call | tf_op jit(solution)/shard_map/stats/pallas_call | solution.py:299
  202.5 0.0 copy-done.5
  202.5 1.0 slice_reduce_fusion.1
  203.5 0.0 copy-start.3
  203.5 22.1 %first.1 = (f32[64,128]{1,0:T(8,128)}, f32[576,64]{1,0:T(8,128)}) custom-call(s32[5]{0:T(128)} %get-tuple-element.78.meta, s32[128]{0:T(128)} %get-tuple-element.77.ids, f32[128,64,128]{2,1,0:T(8,128)} %get-tuple-element.54.hid_ref, f32[128,64,128]{2,1,0:T(8,128)} %get-tuple-element.55.dact_ref, f32[64,128]{1,0:T(8,128)} %stats.2.stat, ...), custom_call_target="tpu_custom_call" | custom-call | tf_op jit(solution)/shard_map/first/pallas_call | solution.py:707
  225.6 1.1 reshape.77
  226.7 1.0 slice_reduce_fusion.2
  227.7 0.1 reshape.79
  227.8 0.0 copy-done.3
  227.8 0.1 reshape.78
  227.9 0.8 select_maximum_fusion
  228.7 22.6 %total.1 = f32[8,4,24,128]{3,2,1,0:T(8,128)} custom-call(f32[8,4,24,128]{3,2,1,0:T(8,128)} %bitcast.49), custom_call_target="tpu_custom_call" | custom-call | tf_op jit(solution)/shard_map/total/pallas_call | solution.py:385
  251.3 1.0 fusion.1
  252.3 0.1 reshape.81
  252.4 0.9 copy.37
  253.3 0.1 reshape.82
  253.4 0.7 reverse_multiply_fusion
  254.2 0.7 slice.72
  254.8 0.1 reshape.84
  254.9 1.1 slice_reduce_fusion.3
  (7 shorter events, 0.1 us)
Async XLA Ops:
  5.0 4.0 %copy-start = (bf16[1,64,128,128]{3,2,1,0:T(8,128)(2,1)S(1)}, bf16[1,64,128,128]{3,2,1,0:T(8,128)(2,1)}, u32[]{:S(2)}) copy-start(bf16[1,64,128,128]{3,2,1,0:T(8,128)(2,1)} %param.9) | copy-start | bytes 6291460
  26.3 6.1 %copy-start.4 = (bf16[9,64,64]{2,1,0:T(8,128)(2,1)S(1)}, bf16[9,64,64]{2,1,0:T(8,128)(2,1)}, u32[]{:S(2)}) copy-start(bf16[9,64,64]{2,1,0:T(8,128)(2,1)} %param.14) | copy-start | bytes 221188
  26.3 6.9 %copy-start.6 = (s32[2]{0:T(128)S(1)}, s32[2]{0:T(128)}, u32[]{:S(2)}) copy-start(s32[2]{0:T(128)} %param.12) | copy-start | bytes 28
  29.4 41.3 %collective-permute-start.1 = (bf16[64,64,128]{2,1,0:T(8,128)(2,1)}, bf16[64,64,128]{2,1,0:T(8,128)(2,1)}, u32[]{:S(2)}, u32[]{:S(2)}) collective-permute-start(bf16[64,64,128]{2,1,0:T(8,128)(2,1)} %get-tuple-element.68), channel_id=1, source_target_pairs={{0,16},{2,18},{4,20},{6,22},{8,24},{10,26},{12,28},{14,30},{16,0},... | collective-permute-start | bytes 3145736 | tf_op jit(solution)/shard_map/ppermute | solution.py:667
  30.5 51.8 %collective-permute-start = (bf16[64,64,128]{2,1,0:T(8,128)(2,1)}, bf16[64,64,128]{2,1,0:T(8,128)(2,1)S(1)}, u32[]{:S(2)}, u32[]{:S(2)}) collective-permute-start(bf16[64,64,128]{2,1,0:T(8,128)(2,1)} %get-tuple-element.69), channel_id=1, source_target_pairs={{0,0},{2,8},{4,16},{6,24},{8,2},{10,10},{12,18},{14,26},{16,4},{18... | collective-permute-start | bytes 3145736 | tf_op jit(solution)/shard_map/ppermute | solution.py:672
  70.7 27.3 %collective-permute-start.2 = (bf16[64,64,128]{2,1,0:T(8,128)(2,1)}, bf16[64,64,128]{2,1,0:T(8,128)(2,1)}, u32[]{:S(2)}, u32[]{:S(2)}) collective-permute-start(bf16[64,64,128]{2,1,0:T(8,128)(2,1)} %collective-permute-done.1), channel_id=1, source_target_pairs={{16,0},{18,8},{20,16},{22,24},{24,2},{26,10},{28,18},{30,26},{0,4}... | collective-permute-start | bytes 3145736 | tf_op jit(solution)/shard_map/ppermute | solution.py:683
  75.1 2.8 %copy-start.2 = (bf16[9,64,64]{2,1,0:T(8,128)(2,1)S(1)}, bf16[9,64,64]{2,1,0:T(8,128)(2,1)}, u32[]{:S(2)}) copy-start(bf16[9,64,64]{2,1,0:T(8,128)(2,1)} %param.13) | copy-start | bytes 221188
  75.1 3.7 %copy-start.7 = (f32[64]{0:T(128)S(1)}, f32[64]{0:T(128)}, u32[]{:S(2)}) copy-start(f32[64]{0:T(128)} %param.15) | copy-start | bytes 772
  75.1 4.4 %copy-start.8 = (f32[64]{0:T(128)S(1)}, f32[64]{0:T(128)}, u32[]{:S(2)}) copy-start(f32[64]{0:T(128)} %param.17) | copy-start | bytes 772
  75.1 5.1 %copy-start.9 = (f32[64]{0:T(128)S(1)}, f32[64]{0:T(128)}, u32[]{:S(2)}) copy-start(f32[64]{0:T(128)} %param.16) | copy-start | bytes 772
  75.1 6.7 %copy-start.10 = (s32[1,512]{1,0:T(1,128)S(1)}, s32[1,512]{1,0:T(1,128)}, u32[]{:S(2)}) copy-start(s32[1,512]{1,0:T(1,128)} %param.11) | copy-start | bytes 6148
  82.3 15.8 %copy-start.1 = (bf16[64,64,128]{2,1,0:T(8,128)(2,1)}, bf16[64,64,128]{2,1,0:T(8,128)(2,1)S(1)}, u32[]{:S(2)}) copy-start(bf16[64,64,128]{2,1,0:T(8,128)(2,1)S(1)} %collective-permute-done.first_ref) | copy-start | bytes 3145732
  179.0 23.4 %copy-start.5 = (f32[64,128]{1,0:T(8,128)S(1)}, f32[64,128]{1,0:T(8,128)}, u32[]{:S(2)}) copy-start(f32[64,128]{1,0:T(8,128)} %get-tuple-element.46.tile_ref) | copy-start | bytes 98308
  203.5 24.3 %copy-start.3 = (f32[576,64]{1,0:T(8,128)S(1)}, f32[576,64]{1,0:T(8,128)}, u32[]{:S(2)}) copy-start(f32[576,64]{1,0:T(8,128)} %get-tuple-element.62) | copy-start | bytes 442372
